TPU v7x, 256 devices: a whole 4x4x8 slice. The times are simulated.
256 devices in a mesh: rep: 16 (over z_lo, x, core), shard: 16 (over y, z_hi).
Axes of the slice: x: 4, y: 4, z: 8 (z_hi: 4, z_lo: 2; z = z_hi * 2 + z_lo), core: 2. Of those that a mesh axis runs over, the one named last changes fastest.
Arguments:
- acts: bfloat16 [32768, 4096], P(('rep', 'shard')), may hold values from -6 to 6
- out_grad: bfloat16 [32768, 2048], P(('rep', 'shard')), may hold values from -6 to 6
- saved_proj: bfloat16 [32768, 2048], P(('rep', 'shard')), may hold values from -6 to 6
- weight: bfloat16 [4096, 2048], P('shard'), may hold values from -0.09375 to 0.09375
- shift_scale: float32 [64, 2, 4096], replicated, may hold values from -3 to 3
- gate: float32 [64, 2048], replicated, may hold values from -4 to 4
- image_of: int32 [32768], P(('rep', 'shard')), may hold values from 0 to 63, never falling along the last dimension, each value on 1 to 2048 neighbouring positions
Outputs:
- acts_grad: bfloat16 [32768, 4096], P(('rep', 'shard'))
- weight_grad: bfloat16 [4096, 2048], P('shard')
- modulation_grad: float32 [64, 2, 4096], replicated
- gate_grad: float32 [64, 2048], replicated
Inputs may be any that keep to these rules, and one draw needn't show every extreme that they name: `image_of`: nondecreasing along the tokens; every image has 1 to 2048 tokens and some image has exactly 2048.
All inputs are finite; a program needn't handle non-finite values.
Results may differ from a plain program's by a relative error of at most 0.0057.
Values may be sent and summed in bfloat16 or wider, within the bound.
A program may use at most 128 MiB of HBM per device.

v0:
```python
import jax
import jax.numpy as jnp
from jax import lax
from jax.sharding import PartitionSpec as P

MEAN_IMG = 512


def on_device(acts, out_grad, saved_proj, weight, shift_scale, gate, image_of):
    rows = acts.shape[0]
    groups = lax.axis_size("shard")
    copies = lax.axis_size("rep")
    total = rows * groups * copies
    images = gate.shape[0]
    highest = lax.Precision.HIGHEST
    values = acts.astype(jnp.float32)
    center = values - jnp.mean(values, axis=1, keepdims=True)
    recip = lax.rsqrt(jnp.mean(center * center, axis=1, keepdims=True) + 1e-06)
    normed = center * recip
    onehot = (image_of[None, :] == jnp.arange(images, dtype=jnp.int32)[:, None]).astype(jnp.float32)
    shift_rows = lax.dot_general(
        onehot, shift_scale[:, 0], (((0,), (0,)), ((), ())), precision=highest
    )
    scale_rows = lax.dot_general(
        onehot, shift_scale[:, 1], (((0,), (0,)), ((), ())), precision=highest
    )
    gate_rows = lax.dot_general(onehot, gate, (((0,), (0,)), ((), ())), precision=highest)
    hidden = (normed * (1.0 + scale_rows) + shift_rows).astype(jnp.bfloat16)
    grad_flat = out_grad.astype(jnp.float32)
    dz = (gate_rows * grad_flat).astype(jnp.bfloat16)
    column_band = lax.all_to_all(hidden, "shard", split_axis=1, concat_axis=0, tiled=True)
    local_grad = lax.dot_general(
        column_band,
        lax.all_gather(dz, "shard", axis=0, tiled=True),
        (((0,), (0,)), ((), ())),
        preferred_element_type=jnp.float32,
    )
    dh = lax.dot_general(
        dz,
        lax.all_gather(weight, "shard", axis=0, tiled=True),
        (((1,), (1,)), ((), ())),
        preferred_element_type=jnp.float32,
    )
    summed = lax.psum(local_grad, "rep")
    weight_grad = (summed * total ** (-0.5)).astype(jnp.bfloat16)
    dnorm = dh * (1.0 + scale_rows)
    acts_grad = recip * (
        dnorm
        - jnp.mean(dnorm, axis=1, keepdims=True)
        - normed * jnp.mean(dnorm * normed, axis=1, keepdims=True)
    )
    factor = MEAN_IMG ** (-0.5)
    shift_part = jnp.dot(onehot, dh, precision=highest) * factor
    scale_part = jnp.dot(onehot, dh * normed, precision=highest) * factor
    gate_part = (
        jnp.dot(onehot, grad_flat * saved_proj.astype(jnp.float32), precision=highest) * factor
    )
    mod_part = jnp.stack([shift_part, scale_part], axis=1)
    modulation_grad, gate_grad = lax.psum((mod_part, gate_part), ("rep", "shard"))
    return (acts_grad.astype(jnp.bfloat16), weight_grad, modulation_grad, gate_grad)


def solution(mesh):
    placed = (
        P(("rep", "shard"), None),
        P(("rep", "shard"), None),
        P(("rep", "shard"), None),
        P("shard", None),
        P(),
        P(),
        P(("rep", "shard")),
    )
    return jax.shard_map(
        on_device,
        mesh=mesh,
        in_specs=placed,
        out_specs=(P(("rep", "shard"), None), P("shard", None), P(), P()),
        check_vma=False,
    )
```

profile of v0, /device:TPU:1, one launch (start us, length us, event | category | flops | bytes accessed | tf_op | source)
XLA Modules:
  0.0 765.2 jit_solution(12941097043454768024)
XLA Ops:
  7.2 1.0 copy-done
  8.2 2.5 fusion.9
  10.8 0.7 all-gather.3.cloned.1.call-update
  11.8 0.4 fusion.15
  12.2 0.9 copy-done.6
  13.1 2.4 fusion.26
  15.5 1.7 convolution_add_fusion.1
  17.2 2.0 fusion
  19.3 57.2 %all_to_all.19 = bf16[128,16,256]{2,0,1:T(8,128)(2,1)S(1)} all-to-all(bf16[128,16,256]{2,0,1:T(8,128)(2,1)S(1)} %bitcast.24), channel_id=1, replica_groups=mesh['rep'=16,'shard'=16] {'shard'}, dimensions={1} | all-to-all | bytes 2097152 | tf_op jit(solution)/shard_map/all_to_all | solution.py:31
  76.5 71.7 %all-gather.5.cloned.1.call-done = bf16[2048,2048]{1,0:T(8,128)(2,1)} async-done(((bf16[128,2048]{1,0:T(8,128)(2,1)}), bf16[2048,2048]{1,0:T(8,128)(2,1)}) %all-gather.5.cloned.1.call-update) | async-done | bytes 8388624 | tf_op jit(solution)/shard_map/all_gather | solution.py:34
  148.2 7.1 fusion.27
  155.5 0.8 copy-done.7
  156.5 1.4 convolution_multiply_fusion.3
  157.9 197.8 %all-gather.3.cloned.1.call-done = bf16[4096,2048]{1,0:T(8,128)(2,1)} async-done(((bf16[256,2048]{1,0:T(8,128)(2,1)}), bf16[4096,2048]{1,0:T(8,128)(2,1)}) %all-gather.3.cloned.1.call-update) | async-done | bytes 16777232 | tf_op jit(solution)/shard_map/all_gather | solution.py:40
  355.8 14.1 %fusion.25 = (f32[128]{0:T(128)S(1)}, f32[128]{0:T(128)S(1)}, f32[128,4096]{1,0:T(8,128)}, f32[128,4096]{1,0:T(8,128)}) fusion(f32[128]{0:T(128)S(1)} %add_rsqrt_fusion, f32[128]{0:T(128)S(1)} %broadcast_multiply_fusion.2, bf16[128,4096]{1,0:T(8,128)(2,1)S(1)} %copy-done.1, f32[128,4096]{1,0:T(8,128)} %copy-done.2, bf16[128,2048]{1,0:T(8,128)(2,1)S(1)} %copy-done.5, ...), kind=kOutput, calls=%fused_computation.43 | convolution fusion | flops 2151153664 | bytes 24643584 | tf_op jit(solution)/shard_map/dot_general | solution.py:38
  369.9 2.6 fusion.1
  372.6 1.2 fusion.2
  373.8 1.5 pad_maximum_fusion
  375.3 109.6 %all-reduce.4.cloned.1.call-done = f32[256,2048]{1,0:T(8,128)} async-done(((f32[256,2048]{1,0:T(8,128)}), f32[256,2048]{1,0:T(8,128)}) %all-reduce.4.cloned.1.call-update) | async-done | bytes 2097168 | tf_op jit(solution)/shard_map/psum | solution.py:44
  484.9 2.9 multiply_convert_fusion
  487.8 1.7 fusion.13
  489.5 263.8 %all-reduce.6.cloned.1.call-done = (f32[64,2,4096]{2,0,1:T(8,128)}, f32[64,2048]{1,0:T(8,128)}) async-done(((f32[64,2,4096]{2,0,1:T(8,128)}, f32[64,2048]{1,0:T(8,128)}), (f32[64,2,4096]{2,0,1:T(8,128)}, f32[64,2048]{1,0:T(8,128)})) %all-reduce.6.cloned.1.call-update) | async-done | bytes 2621456 | tf_op jit(solution)/shard_map/psum | solution.py:59
  753.3 4.6 copy.15
  757.9 0.8 copy.28
  (31 shorter events, 0.9 us)
Async XLA Ops:
  7.2 1.0 copy-start
  7.2 4.4 copy-start.1
  7.2 141.0 %all-gather.5.cloned.1.call-start = ((), (), s32[]{:S(2)}) async-start(), calls=%async_computation.2 | async-start | bytes 8912896 | tf_op jit(solution)/shard_map/all_gather | solution.py:34
  10.7 345.0 %all-gather.3.cloned.1.call-start = ((), (), s32[]{:S(2)}) async-start(), calls=%async_computation.1 | async-start | bytes 17825792 | tf_op jit(solution)/shard_map/all_gather | solution.py:40
  11.5 473.4 %all-reduce.4.cloned.1.call-start = ((), (), s32[]{:S(2)}) async-start(), calls=%async_computation.3 | async-start | bytes 4194304 | tf_op jit(solution)/shard_map/psum | solution.py:44
  11.5 1.6 copy-start.6
  13.1 2.4 copy-start.10
  17.2 2.0 copy-start.2
  155.3 1.0 copy-start.7
  155.3 1.2 copy-start.8
  155.3 200.5 %copy-start.5 = (bf16[128,2048]{1,0:T(8,128)(2,1)S(1)}, bf16[128,2048]{1,0:T(8,128)(2,1)}, u32[]{:S(2)}) copy-start(bf16[128,2048]{1,0:T(8,128)(2,1)} %fusion.9) | copy-start | bytes 1572868
  155.3 598.0 %all-reduce.6.cloned.1.call-start = ((), (), s32[]{:S(2)}) async-start(), calls=%async_computation.4 | async-start | bytes 5242880 | tf_op jit(solution)/shard_map/psum | solution.py:59
  369.9 2.6 copy-start.3
  484.9 2.9 copy-start.4
  753.3 4.6 copy-start.9
Sparse Core Ops, SparseCore 0:
  11.0 137.1 all-gather.4
  150.6 205.0 all-gather.2
  358.4 126.4 all-reduce.3
  490.3 262.9 all-reduce.5
where the time goes:
time: 766 us; the launch traced here: 765 us
  waiting for transfers between devices  644 us (84%)
  blocking collectives  57.2 us (7%)
  matrix products  32.6 us (4%)
  between operations  13.9 us (2%)
  local copies, waits for them, and re-layouts  10.7 us (1%)
    psum x1, waiting for transfers between devices, on_device(): lax.psum((mod_part, gate_part), ('rep', 'shard'))  264 us
    all_gather x1, waiting for transfers between devices, on_device(): lax.all_gather(weight, 'shard', axis=0, tiled=True)  198 us
    psum x1, waiting for transfers between devices, on_device(): summed = lax.psum(local_grad, 'rep')  110 us
    all_gather x1, waiting for transfers between devices, on_device(): lax.all_gather(dz, 'shard', axis=0, tiled=True)  71.7 us
    all_to_all x1, blocking collectives, on_device(): lax.all_to_all(hidden, 'shard', split_axis=1, concat_axis=0, tiled=True)  57.2 us
  transfers between devices with their start and end apart: 4, of which 4 were waited for; matrix products, arithmetic and copies ran while one was open for 5% of the time, Pallas kernels for 0%

commit v1 on v0

v1 whole, which is shorter than its diff:
```python
import jax
import jax.numpy as jnp
from jax import lax
from jax.experimental import pallas as pl
from jax.experimental.pallas import tpu as pltpu
from jax.sharding import PartitionSpec as P

MEAN_IMG = 512
MESH = pl.DeviceIdType.MESH
BF16 = jnp.bfloat16
F32 = jnp.float32
CHUNKS = (
    (0, 384, (0, 1, 2)),
    (384, 384, (1, 2, 0)),
    (768, 256, (2, 0, 1)),
    (1024, 256, (0, 1, 2)),
    (1280, 384, (1, 2, 0)),
    (1664, 384, (2, 0, 1)),
)


def place():
    r = lax.axis_index("rep")
    s = lax.axis_index("shard")
    return (r // 2) % 4, s // 4, (s % 4) * 2 + r // 8, r % 2


def dev(x, y, z, c):
    return ((z % 2) * 8 + x * 2 + c, y * 4 + z // 2)


def band_of(x, y, z, c):
    zb, zh = z % 2, z // 2
    p = (x + c) % 2
    e = (zb + zh) % 2
    step = c * (2 * zb + 3) + (1 - c) * 2 * (1 - e)
    return y + p * (3 - 2 * y), (zh + step) % 4


def flip(pos, bits):
    x, y, z, c = pos
    if bits & 1:
        x = x + 1 - 2 * (x % 2)
    if bits & 2:
        y = y + 1 - 2 * (y % 2)
    if bits & 4:
        z = z + 1 - 2 * (z % 2)
    if bits & 8:
        c = 1 - c
    return x, y, z, c


def cube_index(pos):
    x, y, z, c = pos
    return x % 2 + 2 * (y % 2) + 4 * (z % 2) + 8 * c


def twin(cube, yp, zh):
    cx, cy, cz = cube
    d = (zh - cz + 4) % 4
    c = d % 2
    zb = c * ((3 - d) // 2) + (1 - c) * ((1 + d // 2 + cz) % 2)
    q = (yp // 2 + cy) % 2
    y = yp + q * (3 - 2 * yp)
    return 2 * cx + (q + c) % 2, y, 2 * cz + zb, c


def signal(pos):
    pl.semaphore_signal(
        pltpu.get_barrier_semaphore(), inc=1, device_id=dev(*pos), device_id_type=MESH
    )


def remote(src, dst, ss, rs, pos):
    return pltpu.make_async_remote_copy(
        src_ref=src,
        dst_ref=dst,
        send_sem=ss,
        recv_sem=rs,
        device_id=dev(*pos),
        device_id_type=MESH,
    )


def gather_kernel(
    dz, nrm, gm, w, dz_all, nrm_b, gm_b, w_b,
    dz_s, dz_r, core_s, core_r, nrm_s, nrm_r, gm_s, gm_r, w_s, w_r, loc,
):
    me = place()
    x, y, z, c = me
    zb, zh = z % 2, z // 2
    g = cube_index(me)
    p = (x + c) % 2
    e = (zb + zh) % 2
    yc = y + p * (3 - 2 * y)
    far = (x, yc, (z + (2 * zb - 1) * (3 - 2 * c) + 8) % 8, c)
    near = (x, 3 - y, z, c)
    keeps = (1 - c) * e * (1 - p)
    swaps = (1 - c) * e * p
    sends_far = c + (1 - c) * e

    for k in range(1, 16):
        signal(flip(me, k))
    signal(far)

    @pl.when(swaps == 1)
    def _():
        signal(near)

    pl.semaphore_wait(pltpu.get_barrier_semaphore(), 16 + swaps)

    own = pltpu.make_async_copy(dz, dz_all.at[g], loc.at[0])
    own.start()
    bx, by = band_of(*me)
    own_nrm = pltpu.make_async_copy(
        nrm.at[:, pl.ds(pl.multiple_of((bx * 4 + by) * 256, 256), 256)], nrm_b.at[g], loc.at[1]
    )
    own_nrm.start()
    own_gm = pltpu.make_async_copy(gm.at[bx * 4 + by], gm_b.at[g], loc.at[2])
    own_gm.start()

    copies = {}
    for n, (at, width, order) in enumerate(CHUNKS):
        cols = pl.ds(at, width)
        cp = remote(
            dz.at[:, cols], dz_all.at[g, :, cols], dz_s.at[n, 0], dz_r.at[n, 0],
            flip(me, 1 << order[0]),
        )
        cp.start()
        copies[n, 0] = cp

    to_far = remote(w, w_b, w_s.at[0], w_r, far)
    to_near = remote(w, w_b, w_s.at[1], w_r, near)
    to_self = pltpu.make_async_copy(w, w_b, w_r)

    @pl.when(sends_far == 1)
    def _():
        to_far.start()

    @pl.when(swaps == 1)
    def _():
        to_near.start()

    @pl.when(keeps == 1)
    def _():
        to_self.start()

    small = []
    for k in range(1, 16):
        to = flip(me, k)
        by, bz = band_of(*to)
        b = by * 4 + bz
        cp = remote(
            nrm.at[:, pl.ds(pl.multiple_of(b * 256, 256), 256)], nrm_b.at[g],
            nrm_s.at[k], nrm_r.at[k], to,
        )
        cp.start()
        small.append(cp)
        cp = remote(gm.at[b], gm_b.at[g], gm_s.at[k], gm_r.at[k], to)
        cp.start()
        small.append(cp)

    for n, (at, width, order) in enumerate(CHUNKS):
        cols = pl.ds(at, width)
        one = flip(me, 1 << order[0])
        to = flip(me, 1 << order[1])
        cp = remote(
            dz.at[:, cols], dz_all.at[g, :, cols], dz_s.at[n, 1], dz_r.at[n, 1], to
        )
        cp.start()
        copies[n, 1] = cp
        copies[n, 0].wait_recv()
        slot = dz_all.at[cube_index(one), :, cols]
        cp = remote(slot, slot, dz_s.at[n, 2], dz_r.at[n, 2], to)
        cp.start()
        copies[n, 2] = cp
    for n, (at, width, order) in enumerate(CHUNKS):
        cols = pl.ds(at, width)
        to = flip(me, 1 << order[2])
        cp = remote(
            dz.at[:, cols], dz_all.at[g, :, cols], dz_s.at[n, 3], dz_r.at[n, 3], to
        )
        cp.start()
        copies[n, 3] = cp
        for j, bits in (
            (4, 1 << order[0]),
            (5, 1 << order[1]),
            (6, (1 << order[0]) + (1 << order[1])),
        ):
            if j > 4:
                copies[n, j - 4].wait_recv()
            slot = dz_all.at[cube_index(flip(me, bits)), :, cols]
            cp = remote(slot, slot, dz_s.at[n, j], dz_r.at[n, j], to)
            cp.start()
            copies[n, j] = cp
    own.wait()
    for n, (at, width, order) in enumerate(CHUNKS):
        for j in range(3, 7):
            copies[n, j].wait_recv()
        half = dz_all.at[pl.ds(c * 8, 8), :, pl.ds(at, width)]
        cp = remote(half, half, core_s.at[n], core_r.at[n], flip(me, 8))
        cp.start()
        copies[n, 7] = cp
    for n in range(len(CHUNKS)):
        for j in range(7):
            copies[n, j].wait_send()
        copies[n, 7].wait()
    for cp in small:
        cp.wait()
    own_nrm.wait()
    own_gm.wait()
    to_far.wait_recv()

    @pl.when(sends_far == 1)
    def _():
        to_far.wait_send()

    @pl.when(swaps == 1)
    def _():
        to_near.wait_send()


def gather(dz, nrm, gm, w):
    rows, wide = dz.shape
    n = len(CHUNKS)
    dma = pltpu.SemaphoreType.DMA
    hbm = pl.BlockSpec(memory_space=pl.ANY)
    return pl.pallas_call(
        gather_kernel,
        out_shape=(
            jax.ShapeDtypeStruct((16, rows, wide), BF16),
            jax.ShapeDtypeStruct((16, rows, 256), BF16),
            jax.ShapeDtypeStruct((16, 80, 128), BF16),
            jax.ShapeDtypeStruct(w.shape, BF16),
        ),
        in_specs=[hbm] * 4,
        out_specs=[hbm] * 4,
        scratch_shapes=[
            dma((n, 7)), dma((n, 7)), dma((n,)), dma((n,)),
            dma((16,)), dma((16,)), dma((16,)), dma((16,)),
            dma((2,)), dma, dma((3,)),
        ],
        compiler_params=pltpu.CompilerParams(collective_id=0, has_side_effects=True),
        name="gather_cube",
    )(dz, nrm, gm, w)


def exchange_kernel(dh, msg, dh_full, parts, dh_s, dh_r, ms_s, ms_r, loc):
    me = place()
    x, y, z, c = me
    zb, zh = z % 2, z // 2
    g = cube_index(me)
    by, bz = band_of(*me)
    b = by * 4 + bz
    mine = (1 - c) * ((zb + zh) % 2) * (1 - (x + c) % 2)
    q = x // 2 + 2 * (y // 2) + 4 * zh

    for k in range(1, 16):
        signal(flip(me, k))
    for k in range(16):
        cube = ((x // 2 + k % 2) % 2, (y // 2 + k // 2 % 2) % 2, (zh + k // 4) % 4)
        if k == 0:

            @pl.when(mine == 0)
            def _():
                signal(twin(cube, y, zh))

        else:
            signal(twin(cube, y, zh))
    pl.semaphore_wait(pltpu.get_barrier_semaphore(), 31 - mine)

    own = pltpu.make_async_copy(
        dh.at[g], dh_full.at[:, pl.ds(pl.multiple_of(b * 256, 256), 256)], loc.at[0]
    )
    own.start()
    sends, first = [], None
    for k in range(16):
        hx, hl, hc = (x + k % 4) % 4, (zb + k // 4 % 2) % 2, (c + k // 8) % 2
        piece = msg.at[hx + 4 * hl + 8 * hc]
        to = (hx, by, 2 * bz + hl, hc)
        cp = remote(piece, parts.at[q], ms_s.at[k], ms_r.at[q], to)
        if k == 0:
            first = cp
            keep = pltpu.make_async_copy(piece, parts.at[q], ms_r.at[q])

            @pl.when(mine == 0)
            def _():
                first.start()

            @pl.when(mine == 1)
            def _():
                keep.start()

        else:
            cp.start()
            sends.append(cp)
    blocks = []
    for k in range(1, 16):
        to = flip(me, k)
        cp = remote(
            dh.at[cube_index(to)],
            dh_full.at[:, pl.ds(pl.multiple_of(b * 256, 256), 256)],
            dh_s.at[k], dh_r.at[k], to,
        )
        cp.start()
        blocks.append(cp)
    own.wait()
    for cp in blocks:
        cp.wait()
    for cp in sends:
        cp.wait_send()

    @pl.when(mine == 0)
    def _():
        first.wait_send()

    for k in range(16):
        pltpu.make_async_copy(parts.at[k], parts.at[k], ms_r.at[k]).wait()


def exchange(dh, msg):
    dma = pltpu.SemaphoreType.DMA
    hbm = pl.BlockSpec(memory_space=pl.ANY)
    return pl.pallas_call(
        exchange_kernel,
        out_shape=(
            jax.ShapeDtypeStruct((dh.shape[1], 4096), BF16),
            jax.ShapeDtypeStruct(msg.shape, BF16),
        ),
        in_specs=[hbm] * 2,
        out_specs=[hbm] * 2,
        scratch_shapes=[
            dma((16,)), dma((16,)), dma((16,)), dma((16,)), dma((1,)),
        ],
        compiler_params=pltpu.CompilerParams(collective_id=1, has_side_effects=True),
        name="exchange_parts",
    )(dh, msg)


def spread_kernel(wp, s, w_all, s_all, s1_s, s1_r, w_s, w_r, s2_s, s2_r, co_s, co_r, loc):
    me = place()
    x, y, z, c = me
    zb, zh = z % 2, z // 2
    h = x + 4 * zb + 8 * c
    sib = flip(me, 8)
    plane = [(x, (y + k // 4) % 4, (2 * (zh + k % 4)) % 8 + zb, c) for k in range(1, 16)]
    line = [((x + k % 4) % 4, y, 2 * zh + (zb + k // 4) % 2, c) for k in range(1, 8)]
    for to in plane + line + [sib]:
        signal(to)
    pl.semaphore_wait(pltpu.get_barrier_semaphore(), 23)

    b = y * 4 + zh
    own_s = pltpu.make_async_copy(s, s_all.at[h, b], loc.at[0])
    own_w = pltpu.make_async_copy(wp, w_all.at[h], loc.at[1])
    own_s.start()
    own_w.start()
    firsts = []
    for k, to in enumerate(plane):
        cp = remote(s, s_all.at[h, b], s1_s.at[k], s1_r.at[k], to)
        cp.start()
        firsts.append(cp)
    rest = []
    for k, to in enumerate(line):
        cp = remote(wp, w_all.at[h], w_s.at[k], w_r.at[k], to)
        cp.start()
        rest.append(cp)
    own_s.wait()
    for cp in firsts:
        cp.wait_recv()
    for k, to in enumerate(line):
        cp = remote(s_all.at[h], s_all.at[h], s2_s.at[k], s2_r.at[k], to)
        cp.start()
        rest.append(cp)
    own_w.wait()
    for cp in rest:
        cp.wait_recv()
    half = pl.ds(c * 8, 8)
    last = [
        remote(w_all.at[half], w_all.at[half], co_s.at[0], co_r.at[0], sib),
        remote(s_all.at[half], s_all.at[half], co_s.at[1], co_r.at[1], sib),
    ]
    for cp in last:
        cp.start()
    for cp in firsts + rest:
        cp.wait_send()
    for cp in last:
        cp.wait()


def spread(wp, s):
    dma = pltpu.SemaphoreType.DMA
    hbm = pl.BlockSpec(memory_space=pl.ANY)
    return pl.pallas_call(
        spread_kernel,
        out_shape=(
            jax.ShapeDtypeStruct((16,) + wp.shape, BF16),
            jax.ShapeDtypeStruct((16, 16) + s.shape, BF16),
        ),
        in_specs=[hbm] * 2,
        out_specs=[hbm] * 2,
        scratch_shapes=[
            dma((15,)), dma((15,)), dma((7,)), dma((7,)),
            dma((7,)), dma((7,)), dma((2,)), dma((2,)), dma((2,)),
        ],
        compiler_params=pltpu.CompilerParams(collective_id=2, has_side_effects=True),
        name="spread_sums",
    )(wp, s)


def split_dot(onehot, table):
    hi = table.astype(BF16)
    lo = (table - hi.astype(F32)).astype(BF16)
    dims = (((0,), (0,)), ((), ()))
    return lax.dot_general(onehot, hi, dims, preferred_element_type=F32) + lax.dot_general(
        onehot, lo, dims, preferred_element_type=F32
    )


def on_device(acts, out_grad, saved_proj, weight, shift_scale, gate, image_of):
    rows = acts.shape[0]
    images = gate.shape[0]
    total = rows * lax.axis_size("shard") * lax.axis_size("rep")
    values = acts.astype(F32)
    center = values - jnp.mean(values, axis=1, keepdims=True)
    recip = lax.rsqrt(jnp.mean(center * center, axis=1, keepdims=True) + 1e-06)
    normed = center * recip
    numbers = jnp.arange(images, dtype=jnp.int32)[:, None]
    onehot = (image_of[None, :] == numbers).astype(BF16)
    grad_flat = out_grad.astype(F32)
    dz = (split_dot(onehot, gate) * grad_flat).astype(BF16)
    gate_part = jnp.dot(
        onehot.astype(F32),
        grad_flat * saved_proj.astype(F32),
        precision=lax.Precision.HIGHEST,
    )
    gm = gate_part.astype(BF16).reshape(images, 16, 128).transpose(1, 0, 2)
    ids = jnp.broadcast_to(image_of.astype(BF16)[None, None, :], (16, 16, 128))
    gm = jnp.concatenate([gm, ids], axis=1)
    dz_all, nrm_b, gm_b, w_b = gather(dz, normed.astype(BF16), gm, weight)

    by, bz = band_of(*place())
    band = by * 4 + bz
    dz_all = dz_all.reshape(16 * rows, -1)
    nrm_b = nrm_b.reshape(16 * rows, 256)
    cube_ids = gm_b[:, images, :].reshape(1, 16 * rows)
    cube_hot = (cube_ids == numbers.astype(BF16)).astype(BF16)
    table = lax.dynamic_slice_in_dim(shift_scale, band * 256, 256, axis=2).reshape(images, 512)
    mods = split_dot(cube_hot, table)
    nrm_f = nrm_b.astype(F32)
    hidden = (nrm_f * (1.0 + mods[:, 256:]) + mods[:, :256]).astype(BF16)
    wg = lax.dot_general(
        hidden, dz_all, (((0,), (0,)), ((), ())), preferred_element_type=F32
    ).astype(BF16)
    dh = lax.dot_general(dz_all, w_b, (((1,), (1,)), ((), ())), preferred_element_type=F32)
    both = jnp.concatenate([dh, dh * nrm_f], axis=1)
    hi = both.astype(BF16)
    lo = (both - hi.astype(F32)).astype(BF16)
    sums = jnp.dot(cube_hot, hi, preferred_element_type=F32) + jnp.dot(
        cube_hot, lo, preferred_element_type=F32
    )
    gate_sum = jnp.sum(gm_b[:, :images, :].astype(F32), axis=0)
    mod_piece = sums.astype(BF16).reshape(16, 16, 128)
    gate_piece = jnp.pad(gate_sum.astype(BF16).reshape(16, 4, 128), ((0, 0), (0, 12), (0, 0)))
    msg = jnp.concatenate([wg.reshape(16, 16, -1), mod_piece, gate_piece], axis=2)
    dh_full, parts = exchange(dh.astype(BF16).reshape(16, rows, 256), msg)

    red = jnp.sum(parts.astype(F32), axis=0)
    wp = (red[:, :2048] * total ** (-0.5)).astype(BF16)
    s = (red[:, 2048:] * MEAN_IMG ** (-0.5)).astype(BF16)
    w_all, s_all = spread(wp, s)

    scale_rows = split_dot(onehot, shift_scale[:, 1])
    dnorm = dh_full.astype(F32) * (1.0 + scale_rows)
    acts_grad = recip * (
        dnorm
        - jnp.mean(dnorm, axis=1, keepdims=True)
        - normed * jnp.mean(dnorm * normed, axis=1, keepdims=True)
    )
    mod = s_all[..., :128].reshape(16, 16, 4, 2, 2, 128).transpose(0, 2, 3, 1, 4, 5)
    modulation_grad = mod.reshape(images, 2, -1).astype(F32)
    gate_grad = s_all[:, :, :4, 128:].transpose(0, 2, 1, 3).reshape(images, -1).astype(F32)
    return (
        acts_grad.astype(BF16),
        w_all.reshape(256, -1),
        modulation_grad,
        gate_grad,
    )


def solution(mesh):
    placed = (
        P(("rep", "shard"), None),
        P(("rep", "shard"), None),
        P(("rep", "shard"), None),
        P("shard", None),
        P(),
        P(),
        P(("rep", "shard")),
    )
    return jax.shard_map(
        on_device,
        mesh=mesh,
        in_specs=placed,
        out_specs=(P(("rep", "shard"), None), P("shard", None), P(), P()),
        check_vma=False,
    )
```

time: 766 us -> 176 us (0.23)
  waiting for transfers between devices: 644 us -> 0 us
  Pallas kernels: 0 us -> 136 us
  blocking collectives: 57.2 us -> 0 us
  matrix products: 32.6 us -> 13.2 us
  between operations: 13.9 us -> 1.06 us
    psum x2 -> x0, waiting for transfers between devices: 373 us -> none  [the longest x1 264 us: on_device(): lax.psum((mod_part, gate_part), ('rep', 'shard'))]
    all_gather x2 -> x0, waiting for transfers between devices: 270 us -> none  [the longest x1 198 us: on_device(): lax.all_gather(weight, 'shard', axis=0, tiled=True)]
    pallas_call x0 -> x3, Pallas kernels: none -> 136 us  [the longest x1 66.1 us: gather(): pl.pallas_call(gather_kernel, out_shape=(jax.ShapeDtypeStruct((16, rows,...]
    all_to_all x1 -> x0, blocking collectives: 57.2 us -> none  [on_device(): lax.all_to_all(hidden, 'shard', split_axis=1, concat_axis=0, tiled=True)]
    dot_general x8 -> x11, matrix products: 32.6 us -> 13.2 us  [the longest x1 3.59 us: on_device(): lax.dot_general(dz_all, w_b, (((1,), (1,)), ((), ())), preferred_element_...]
  transfers between devices with their start and end apart: 4 -> 0, of which waited for: 4 -> 0; matrix products, arithmetic and copies ran while one was open for 5% -> 0% of each run, Pallas kernels for 0% -> 0%
where the time goes in v1:
time: 176 us
  Pallas kernels  136 us (77%)
  matrix products  13.2 us (8%)
  local copies, waits for them, and re-layouts  12.6 us (7%)
  other arithmetic  12.3 us (7%)
    pallas_call x1, Pallas kernels, gather(): pl.pallas_call(gather_kernel, out_shape=(jax.ShapeDtypeStruct((16, rows,...  66.1 us
    pallas_call x1, Pallas kernels, exchange(): pl.pallas_call(exchange_kernel, out_shape=(jax.ShapeDtypeStruct((dh.shape...  36.9 us
    pallas_call x1, Pallas kernels, spread(): pl.pallas_call(spread_kernel, out_shape=(jax.ShapeDtypeStruct((16,) + wp....  33.4 us
    unnamed x27, local copies, waits for them, and re-layouts  4.96 us
    convert_element_type x2, local copies, waits for them, and re-layouts, on_device(): modulation_grad = mod.reshape(images, 2, -1).astype(F32)  4.54 us
    dot_general x1, matrix products, on_device(): lax.dot_general(dz_all, w_b, (((1,), (1,)), ((), ())), preferred_element_...  3.59 us

profile of v1, /device:TPU:1, one launch (start us, length us, event | category | flops | bytes accessed | tf_op | source)
XLA Modules:
  0.0 175.6 jit_solution(9340655038461062942)
XLA Ops:
  0.8 1.0 constant_dynamic-slice_fusion
  1.8 1.5 convert_reduce_fusion
  3.8 1.3 fusion.7.nrm
  5.5 1.1 fusion.9.dz
  8.1 66.1 %gather_cube.1 = (bf16[16,128,2048]{2,1,0:T(8,128)(2,1)}, bf16[16,128,256]{2,1,0:T(8,128)(2,1)}, bf16[16,80,128]{2,1,0:T(8,128)(2,1)}, bf16[256,2048]{1,0:T(8,128)(2,1)}) custom-call(bf16[128,2048]{1,0:T(8,128)(2,1)} %fusion.9.dz, bf16[128,4096]{1,0:T(8,128)(2,1)} %fusion.7.nrm, bf16[16,80,128]{2,1,0:T(8,128)(2,1)} %pad_maximum_fusion.1.gm, bf16[256,2048]{1,0:T(8,128)(2,1)} %w.1), custom_call_target="tpu_custom_call" | custom-call | tf_op jit(solution)/shard_map/gather_cube/pallas_call | solution.py:228
  75.1 0.8 fusion.32
  75.9 0.8 convolution_add_fusion.1
  76.7 2.6 %copy-done.1 = bf16[16,128,2048]{2,1,0:T(8,128)(2,1)S(1)} copy-done((bf16[16,128,2048]{2,1,0:T(8,128)(2,1)S(1)}, bf16[16,128,2048]{2,1,0:T(8,128)(2,1)}, u32[]{:S(2)}) %copy-start.1) | copy-done | bytes 8388632
  79.4 2.5 %convolution_convert_fusion = bf16[256,2048]{1,0:T(8,128)(2,1)S(1)} fusion(bf16[2048,2048]{1,0:T(8,128)(2,1)S(1)} %bitcast.47, bf16[2048,256]{1,0:T(8,128)(2,1)S(1)} %bitcast.56, f32[2048,512]{1,0:T(8,128)S(1)} %convolution_add_fusion.1), kind=kOutput, calls=%fused_computation.11 | convolution fusion | flops 2150629376 | bytes 14680064 | tf_op jit(solution)/shard_map/dot_general | solution.py:451
  81.8 3.6 %convert_multiply_fusion = (f32[2048,256]{1,0:T(8,128)S(1)}, bf16[2048,256]{1,0:T(8,128)(2,1)}, f32[2048,256]{1,0:T(8,128)S(1)}) fusion(bf16[16,128,256]{2,1,0:T(8,128)(2,1)S(1)} %copy-done.6, bf16[2048,2048]{1,0:T(8,128)(2,1)S(1)} %bitcast.48, bf16[256,2048]{1,0:T(8,128)(2,1)S(1)} %copy-done.7), kind=kOutput, calls=%fused_computation.7 | convolution fusion | flops 2149056512 | bytes 15728640 | tf_op jit(solution)/shard_map/dot_general | solution.py:454
  87.0 1.1 fusion.21.msg
  88.1 36.9 %exchange_parts.1 = (bf16[128,4096]{1,0:T(8,128)(2,1)}, bf16[16,16,2304]{2,1,0:T(8,128)(2,1)}) custom-call(bf16[16,128,256]{2,1,0:T(8,128)(2,1)} %bitcast.49, bf16[16,16,2304]{2,1,0:T(8,128)(2,1)} %fusion.21.msg), custom_call_target="tpu_custom_call" | custom-call | tf_op jit(solution)/shard_map/exchange_parts/pallas_call | solution.py:324
  125.0 1.4 convert_reduce_fusion.1
  127.7 33.4 %spread_sums.1 = (bf16[16,16,2048]{2,1,0:T(8,128)(2,1)}, bf16[16,16,16,256]{3,2,1,0:T(8,128)(2,1)}) custom-call(bf16[16,2048]{1,0:T(8,128)(2,1)} %fusion.36.wp, bf16[16,256]{1,0:T(8,128)(2,1)} %fusion.50.s), custom_call_target="tpu_custom_call" | custom-call | tf_op jit(solution)/shard_map/spread_sums/pallas_call | solution.py:393
  161.1 1.4 slice_convert_fusion
  162.5 1.1 copy.14
  163.7 3.4 %reshape.81 = f32[64,2,4096]{2,1,0:T(2,128)} reshape(f32[16,4,2,16,2,128]{5,4,3,2,1,0:T(2,128)S(1)} %copy.14) | data formatting | bytes 4194304 | tf_op jit(solution)/shard_map/convert_element_type | solution.py:480
  167.1 1.3 convert_bitcast_fusion
  168.4 1.0 copy.33
  169.4 1.1 slice.31
  170.5 0.8 fusion.34
  171.4 1.5 fusion.59
  172.8 1.7 fusion.16
  174.6 1.0 copy.36
  (43 shorter events, 5.9 us)
Async XLA Ops:
  0.6 2.7 %copy-start = (bf16[128,4096]{1,0:T(8,128)(2,1)S(1)}, bf16[128,4096]{1,0:T(8,128)(2,1)}, u32[]{:S(2)}) copy-start(bf16[128,4096]{1,0:T(8,128)(2,1)} %param.7) | copy-start | bytes 3145732
  1.8 3.3 %copy-start.3 = (f32[64,2048]{1,0:T(8,128)S(1)}, f32[64,2048]{1,0:T(8,128)}, u32[]{:S(2)}) copy-start(f32[64,2048]{1,0:T(8,128)} %param.12) | copy-start | bytes 1572868
  1.8 3.3 %copy-start.11 = (s32[128]{0:T(128)S(1)}, s32[128]{0:T(128)}, u32[]{:S(2)}) copy-start(s32[128]{0:T(128)} %param.13) | copy-start | bytes 1540
  3.8 1.7 copy-start.2
  5.1 1.5 copy-start.9
  75.0 1.7 copy-start.6
  75.9 3.5 %copy-start.1 = (bf16[16,128,2048]{2,1,0:T(8,128)(2,1)S(1)}, bf16[16,128,2048]{2,1,0:T(8,128)(2,1)}, u32[]{:S(2)}) copy-start(bf16[16,128,2048]{2,1,0:T(8,128)(2,1)} %get-tuple-element.12) | copy-start | bytes 25165828
  79.4 2.5 %copy-start.7 = (bf16[256,2048]{1,0:T(8,128)(2,1)S(1)}, bf16[256,2048]{1,0:T(8,128)(2,1)}, u32[]{:S(2)}) copy-start(bf16[256,2048]{1,0:T(8,128)(2,1)} %get-tuple-element.13) | copy-start | bytes 3145732
  86.0 1.0 copy-start.10
  167.1 2.3 %copy-start.8 = (f32[64,2,4096]{2,1,0:T(2,128)S(1)}, f32[64,2,4096]{2,1,0:T(2,128)}, u32[]{:S(2)}) copy-start(f32[64,2,4096]{2,1,0:T(2,128)} %param.11) | copy-start | bytes 6291460
  169.4 2.0 %copy-start.5 = (bf16[128,4096]{1,0:T(8,128)(2,1)S(1)}, bf16[128,4096]{1,0:T(8,128)(2,1)}, u32[]{:S(2)}) copy-start(bf16[128,4096]{1,0:T(8,128)(2,1)} %get-tuple-element.16) | copy-start | bytes 3145732
  172.8 1.7 copy-start.4

commit v2 on v0

v2 whole, which is shorter than its diff:
```python
import jax
import jax.numpy as jnp
from jax import lax
from jax.experimental import pallas as pl
from jax.experimental.pallas import tpu as pltpu
from jax.sharding import PartitionSpec as P

MEAN_IMG = 512
MESH = pl.DeviceIdType.MESH
BF16 = jnp.bfloat16
F32 = jnp.float32
CHUNKS = (
    (0, 384, (0, 1, 2)),
    (384, 384, (1, 2, 0)),
    (768, 256, (2, 0, 1)),
    (1024, 256, (0, 1, 2)),
    (1280, 384, (1, 2, 0)),
    (1664, 384, (2, 0, 1)),
)


def place():
    r = lax.axis_index("rep")
    s = lax.axis_index("shard")
    return (r // 2) % 4, s // 4, (s % 4) * 2 + r // 8, r % 2


def dev(x, y, z, c):
    return ((z % 2) * 8 + x * 2 + c, y * 4 + z // 2)


def band_of(x, y, z, c):
    zb, zh = z % 2, z // 2
    p = (x + c) % 2
    e = (zb + zh) % 2
    step = c * (2 * zb + 3) + (1 - c) * 2 * (1 - e)
    return y + p * (3 - 2 * y), (zh + step) % 4


def flip(pos, bits):
    x, y, z, c = pos
    if bits & 1:
        x = x + 1 - 2 * (x % 2)
    if bits & 2:
        y = y + 1 - 2 * (y % 2)
    if bits & 4:
        z = z + 1 - 2 * (z % 2)
    if bits & 8:
        c = 1 - c
    return x, y, z, c


def cube_index(pos):
    x, y, z, c = pos
    return x % 2 + 2 * (y % 2) + 4 * (z % 2) + 8 * c


def twin(cube, yp, zh):
    cx, cy, cz = cube
    d = (zh - cz + 4) % 4
    c = d % 2
    zb = c * ((3 - d) // 2) + (1 - c) * ((1 + d // 2 + cz) % 2)
    q = (yp // 2 + cy) % 2
    y = yp + q * (3 - 2 * yp)
    return 2 * cx + (q + c) % 2, y, 2 * cz + zb, c


def signal(pos):
    pl.semaphore_signal(
        pltpu.get_barrier_semaphore(), inc=1, device_id=dev(*pos), device_id_type=MESH
    )


def remote(src, dst, ss, rs, pos):
    return pltpu.make_async_remote_copy(
        src_ref=src,
        dst_ref=dst,
        send_sem=ss,
        recv_sem=rs,
        device_id=dev(*pos),
        device_id_type=MESH,
    )


def dot(a, b, dims):
    return lax.dot_general(a, b, (dims, ((), ())), preferred_element_type=F32)


def two_terms(v):
    hi = v.astype(BF16)
    return hi, (v - hi.astype(F32)).astype(BF16)


def image_hot(ids, count):
    rows = lax.broadcasted_iota(jnp.int32, (count, ids.shape[1]), 0).astype(F32)
    return jnp.where(rows == ids, 1.0, 0.0)


def block_kernel(
    acts, og, sp, w, ss, gate, ids,
    o_acts, o_w, o_mod, o_gate,
    acts_v, og_v, sp_v, gate_v, ss_v, ss_b, rm, st, dz_all, acts_b, st_b, gm, gm_b, w_b,
    hid, nrm, dh, dh_b, msg_w, msg_s, part_w, part_s, dh_full, sc1, wp, s_own, s1, s_mod, gd,
    o2, v2,
    dz_s, dz_r, core_s, core_r, ac_s, ac_r, st_s, st_r, gm_s, gm_r, w_s, w_r,
    dh_s, dh_r, mw_s, mw_r, ms_s, ms_r, s1_s, s1_r, wp_s, wp_r, sm_s, sm_r, gd_s, gd_r,
    co_s, co_r, loc,
):
    me = place()
    x, y, z, c = me
    zb, zh = z % 2, z // 2
    g = cube_index(me)
    p = (x + c) % 2
    e = (zb + zh) % 2
    far = (x, y + p * (3 - 2 * y), (z + (2 * zb - 1) * (3 - 2 * c) + 8) % 8, c)
    near = (x, 3 - y, z, c)
    keeps = (1 - c) * e * (1 - p)
    swaps = (1 - c) * e * p
    sends_far = c + (1 - c) * e
    by, bz = band_of(*me)
    b = by * 4 + bz
    mine = keeps
    q = x // 2 + 2 * (y // 2) + 4 * zh
    h = x + 4 * zb + 8 * c
    kept = y * 4 + zh
    sib = flip(me, 8)
    plane = [(x, (y + k // 4) % 4, (2 * (zh + k % 4)) % 8 + zb, c) for k in range(1, 16)]
    line = [((x + k % 4) % 4, y, 2 * zh + (zb + k // 4) % 2, c) for k in range(1, 8)]
    band_cols = pl.ds(pl.multiple_of(b * 256, 256), 256)

    loads = [
        pltpu.make_async_copy(a, v, loc.at[i])
        for i, (a, v) in enumerate(
            ((og, og_v), (gate, gate_v), (acts, acts_v), (sp, sp_v),
             (ss.at[:, :, band_cols], ss_b), (ss, ss_v), (acts.at[:, band_cols], acts_b.at[g]))
        )
    ]
    for cp in loads:
        cp.start()
    for k in range(1, 16):
        signal(flip(me, k))
    signal(far)

    @pl.when(swaps == 1)
    def _():
        signal(near)

    for k in range(16):
        cube = ((x // 2 + k % 2) % 2, (y // 2 + k // 2 % 2) % 2, (zh + k // 4) % 4)
        if k == 0:

            @pl.when(mine == 0)
            def _():
                signal(twin(cube, y, zh))

        else:
            signal(twin(cube, y, zh))
    for to in plane + line:
        signal(to)

    ids_f = ids[...].astype(F32)
    hot = image_hot(ids_f, 128)
    hot_t = hot.T[:, :64].astype(BF16)
    loads[0].wait()
    loads[1].wait()
    for j in range(0, 2048, 512):
        cols = slice(j, j + 512)
        hi, lo = two_terms(gate_v[:, cols])
        rows = dot(hot_t, hi, ((1,), (0,))) + dot(hot_t, lo, ((1,), (0,)))
        dz_all[g, :, cols] = (rows * og_v[:, cols].astype(F32)).astype(BF16)

    pl.semaphore_wait(pltpu.get_barrier_semaphore(), 54 + swaps - mine)

    copies = {}

    def relay(n, j, bits, to):
        at, width, _ = CHUNKS[n]
        slot = dz_all.at[cube_index(flip(me, bits)), :, pl.ds(at, width)]
        cp = remote(slot, slot, dz_s.at[n, j], dz_r.at[n, j], to)
        cp.start()
        copies[n, j] = cp

    for n, (_, _, order) in enumerate(CHUNKS):
        relay(n, 0, 0, flip(me, 1 << order[0]))

    to_far = remote(w, w_b, w_s.at[0], w_r, far)
    to_near = remote(w, w_b, w_s.at[1], w_r, near)
    to_self = pltpu.make_async_copy(w, w_b, w_r)

    @pl.when(sends_far == 1)
    def _():
        to_far.start()

    @pl.when(swaps == 1)
    def _():
        to_near.start()

    @pl.when(keeps == 1)
    def _():
        to_self.start()

    loads[2].wait()

    def stats(i, _):
        rows = pl.ds(pl.multiple_of(i * 16, 16), 16)
        v = acts_v[rows, :].astype(F32)
        m = jnp.mean(v, axis=1, keepdims=True)
        v = v - m
        r = lax.rsqrt(jnp.mean(v * v, axis=1, keepdims=True) + 1e-06)
        lane = lax.broadcasted_iota(jnp.int32, (16, 128), 1)
        rm[rows, :] = jnp.where(lane == 0, r, jnp.where(lane == 1, m, 0.0))
        return 0

    lax.fori_loop(0, 8, stats, 0)
    turned = rm[...].T[:8, :]
    row = lax.broadcasted_iota(jnp.int32, (8, 128), 0)
    st[...] = jnp.where(row == 2, ids_f, turned)
    st_b[g] = st[...]

    for n, (_, _, order) in enumerate(CHUNKS):
        to = flip(me, 1 << order[1])
        relay(n, 1, 0, to)
        copies[n, 0].wait_recv()
        relay(n, 2, 1 << order[0], to)

    blocks = []
    for k in range(1, 16):
        to = flip(me, k)
        ty, tz = band_of(*to)
        cols = pl.ds(pl.multiple_of((ty * 4 + tz) * 256, 256), 256)
        blocks.append(remote(st, st_b.at[g], st_s.at[k], st_r.at[k], to))
        blocks.append(remote(acts.at[:, cols], acts_b.at[g], ac_s.at[k], ac_r.at[k], to))
    for cp in blocks:
        cp.start()

    for n, (_, _, order) in enumerate(CHUNKS):
        to = flip(me, 1 << order[2])
        one, two = 1 << order[0], 1 << order[1]
        relay(n, 3, 0, to)
        relay(n, 4, one, to)
        copies[n, 1].wait_recv()
        relay(n, 5, two, to)
        copies[n, 2].wait_recv()
        relay(n, 6, one + two, to)

    loads[3].wait()
    hot_b = hot[:64].astype(BF16)
    for j in range(0, 2048, 512):
        cols = slice(j, j + 512)
        hi, lo = two_terms(og_v[:, cols].astype(F32) * sp_v[:, cols].astype(F32))
        gm[:, cols] = (dot(hot_b, hi, ((1,), (0,))) + dot(hot_b, lo, ((1,), (0,)))).astype(BF16)
    gm_b[g] = gm[:, pl.ds(pl.multiple_of(b * 128, 128), 128)]
    gates = []
    for k in range(1, 16):
        to = flip(me, k)
        ty, tz = band_of(*to)
        cols = pl.ds(pl.multiple_of((ty * 4 + tz) * 128, 128), 128)
        cp = remote(gm.at[:, cols], gm_b.at[g], gm_s.at[k], gm_r.at[k], to)
        cp.start()
        gates.append(cp)

    loads[5].wait()

    def scales(j, _):
        cols = pl.ds(pl.multiple_of(j * 512, 512), 512)
        hi, lo = two_terms(ss_v[:, 1, cols])
        sc1[:, cols] = 1.0 + (dot(hot_t, hi, ((1,), (0,))) + dot(hot_t, lo, ((1,), (0,))))
        return 0

    lax.fori_loop(0, 8, scales, 0)

    loads[4].wait()
    loads[6].wait()
    for cp in blocks:
        cp.wait_recv()
    shift_hi, shift_lo = two_terms(ss_b[:, 0, :])
    scale_hi, scale_lo = two_terms(ss_b[:, 1, :])
    tables = jnp.concatenate(
        [
            jnp.concatenate([shift_hi, scale_hi], axis=1),
            jnp.concatenate([shift_lo, scale_lo], axis=1),
        ],
        axis=0,
    )

    def modulate(t, _):
        block = st_b[t]
        wide = jnp.concatenate([block, jnp.zeros((120, 128), F32)], axis=0).T
        r, m = wide[:, 0:1], wide[:, 1:2]
        own = image_hot(block[2:3], 64)
        twice = jnp.concatenate([own, own], axis=0).T.astype(BF16)
        mods = dot(twice, tables, ((1,), (0,)))
        normed = (acts_b[t].astype(F32) - m) * r
        nrm[t] = normed
        out = normed * (1.0 + mods[:, 256:]) + mods[:, :256]
        hid[:, pl.ds(pl.multiple_of(t * 128, 128), 128)] = out.T.astype(BF16)
        rows = lax.broadcasted_iota(jnp.int32, (128, 128), 0)
        hit = ((rows // 2).astype(F32) == block[2:3])
        o2[:, pl.ds(pl.multiple_of(t * 128, 128), 128)] = jnp.where(
            hit & (rows % 2 == 0), 1.0, 0.0
        ).astype(BF16)
        o2[:, pl.ds(pl.multiple_of(2048 + t * 128, 128), 128)] = jnp.where(
            hit & (rows % 2 == 1), 1.0, 0.0
        ).astype(BF16)
        return 0

    lax.fori_loop(0, 16, modulate, 0)

    parts, first = [], []
    for half in range(2):
        for n in range(3 * half, 3 * half + 3):
            at, width, _ = CHUNKS[n]
            for j in range(3, 7):
                copies[n, j].wait_recv()
            slots = dz_all.at[pl.ds(c * 8, 8), :, pl.ds(at, width)]
            cp = remote(slots, slots, core_s.at[n], core_r.at[n], sib)
            cp.start()
            copies[n, 7] = cp
        for n in range(3 * half, 3 * half + 3):
            copies[n, 7].wait_recv()
        lo = half * 1024

        def grads(j, _):
            cols = pl.ds(pl.multiple_of(lo + j * 256, 256), 256)
            v = dot(hid[...], dz_all[:, :, cols].reshape(2048, 256), ((1,), (0,)))
            msg_w[:, :, cols] = v.astype(BF16).reshape(16, 16, 256)
            return 0

        lax.fori_loop(0, 4, grads, 0)
        for k in range(16):
            hx, hl, hc = (x + k % 4) % 4, (zb + k // 4 % 2) % 2, (c + k // 8) % 2
            cols = pl.ds(lo, 1024)
            piece = msg_w.at[hx + 4 * hl + 8 * hc, :, cols]
            to = (hx, by, 2 * bz + hl, hc)
            into = part_w.at[q, :, cols]
            cp = remote(piece, into, mw_s.at[half, k], mw_r.at[half, q], to)
            if k == 0:
                keep = pltpu.make_async_copy(piece, into, mw_r.at[half, q])
                first.append(cp)

                @pl.when(mine == 0)
                def _():
                    cp.start()

                @pl.when(mine == 1)
                def _():
                    keep.start()

            else:
                cp.start()
                parts.append(cp)
        if half == 0:
            to_far.wait_recv()

        def back(t, _):
            rows = pl.ds(t * 4, 4)
            v = dot(
                dz_all[rows, :, lo : lo + 1024].reshape(512, 1024),
                w_b[:, lo : lo + 1024],
                ((1,), (1,)),
            ).reshape(4, 128, 256)
            if half == 0:
                dh[rows] = v
            else:
                v = v + dh[rows]
                dh[rows] = v
                dh_b[rows] = v.astype(BF16)
            return 0

        lax.fori_loop(0, 4, back, 0)

    grad_cols = band_cols
    dh_full[:, grad_cols] = dh_b[g]
    for k in range(1, 16):
        to = flip(me, k)
        cp = remote(
            dh_b.at[cube_index(to)], dh_full.at[:, grad_cols], dh_s.at[k], dh_r.at[k], to
        )
        cp.start()
        gates.append(cp)

    def products(t, _):
        v2[t] = (dh[t] * nrm[t]).astype(BF16)
        return 0

    lax.fori_loop(0, 16, products, 0)
    sums = dot(o2[:, :2048], dh_b[...].reshape(2048, 256), ((1,), (0,)))
    sums = sums + dot(o2[:, 2048:], v2[...].reshape(2048, 256), ((1,), (0,)))
    for cp in gates[:15]:
        cp.wait_recv()
    gate_sum = gm_b[0].astype(F32)
    for t in range(1, 16):
        gate_sum = gate_sum + gm_b[t].astype(F32)
    at_row = lax.broadcasted_iota(jnp.int32, (256, 64), 0)
    image = lax.broadcasted_iota(jnp.int32, (256, 64), 1)
    put = (at_row % 16 < 4) & (image == at_row // 16 * 4 + at_row % 16)
    spaced = dot(
        jnp.where(put, 1.0, 0.0).astype(BF16), gate_sum.astype(BF16), ((1,), (0,))
    ).astype(BF16)
    for i in range(16):
        rows = slice(8 * i, 8 * i + 8)
        msg_s[i, 0] = jnp.concatenate([sums[rows, :128], sums[rows, 128:]], axis=0).astype(BF16)
        msg_s[i, 1] = spaced[16 * i : 16 * i + 16]
    for k in range(16):
        hx, hl, hc = (x + k % 4) % 4, (zb + k // 4 % 2) % 2, (c + k // 8) % 2
        piece = msg_s.at[hx + 4 * hl + 8 * hc]
        to = (hx, by, 2 * bz + hl, hc)
        cp = remote(piece, part_s.at[q], ms_s.at[k], ms_r.at[q], to)
        if k == 0:
            keep_s = pltpu.make_async_copy(piece, part_s.at[q], ms_r.at[q])
            first.append(cp)

            @pl.when(mine == 0)
            def _():
                cp.start()

            @pl.when(mine == 1)
            def _():
                keep_s.start()

        else:
            cp.start()
            parts.append(cp)

    rest = []
    for half in range(2):
        cols = slice(half * 1024, half * 1024 + 1024)
        for k in range(16):
            into = part_w.at[k, :, cols]
            pltpu.make_async_copy(into, into, mw_r.at[half, k]).wait()
        total = part_w[0, :, cols].astype(F32)
        for k in range(1, 16):
            total = total + part_w[k, :, cols].astype(F32)
        wp[:, cols] = (total * 32768 ** (-0.5)).astype(BF16)
    own_w = pltpu.make_async_copy(wp, o_w.at[h], loc.at[0])
    own_w.start()
    for k, to in enumerate(line):
        cp = remote(wp, o_w.at[h], wp_s.at[k], wp_r.at[k], to)
        cp.start()
        rest.append(cp)

    for k in range(16):
        pltpu.make_async_copy(part_s.at[k], part_s.at[k], ms_r.at[k]).wait()
    total = part_s[0].astype(F32)
    for k in range(1, 16):
        total = total + part_s[k].astype(F32)
    s_own[...] = (total * MEAN_IMG ** (-0.5)).astype(BF16)
    s1[kept] = s_own[...]
    firsts = []
    for k, to in enumerate(plane):
        cp = remote(s_own, s1.at[kept], s1_s.at[k], s1_r.at[k], to)
        cp.start()
        firsts.append(cp)

    for cp in gates[15:]:
        cp.wait_recv()

    def finish(i, _):
        rows = pl.ds(pl.multiple_of(i * 16, 16), 16)
        r, m = rm[rows, 0:1], rm[rows, 1:2]
        normed = (acts_v[rows, :].astype(F32) - m) * r
        dn = dh_full[rows, :].astype(F32) * sc1[rows, :]
        mean = jnp.mean(dn, axis=1, keepdims=True)
        along = jnp.mean(dn * normed, axis=1, keepdims=True)
        o_acts[rows, :] = (r * (dn - mean - normed * along)).astype(BF16)
        return 0

    lax.fori_loop(0, 4, finish, 0)
    for cp in firsts:
        cp.wait_recv()
    s_mod[h] = s1[:, 0]
    gd[h] = jnp.concatenate([s1[k, 1].astype(F32)[:4] for k in range(16)], axis=0).astype(BF16)
    for k, to in enumerate(line):
        for v, ss_, rs_ in ((s_mod, sm_s, sm_r), (gd, gd_s, gd_r)):
            cp = remote(v.at[h], v.at[h], ss_.at[k], rs_.at[k], to)
            cp.start()
            rest.append(cp)
    lax.fori_loop(4, 8, finish, 0)

    own_w.wait()
    for cp in rest[:7]:
        cp.wait_recv()
    mates = pl.ds(c * 8, 8)
    last = [remote(o_w.at[mates], o_w.at[mates], co_s.at[0], co_r.at[0], sib)]
    last[0].start()
    for cp in rest[7:]:
        cp.wait_recv()
    for i, v in ((1, s_mod), (2, gd)):
        cp = remote(v.at[mates], v.at[mates], co_s.at[i], co_r.at[i], sib)
        cp.start()
        last.append(cp)
    last[1].wait_recv()
    last[2].wait_recv()

    def write(i, _):
        images = pl.ds(i * 4, 4)
        for k in range(16):
            v = s_mod[i, k].astype(F32)
            o_mod[images, :, k * 256 : k * 256 + 128] = v[:8].reshape(4, 2, 128)
            o_mod[images, :, k * 256 + 128 : k * 256 + 256] = v[8:].reshape(4, 2, 128)
        return 0

    lax.fori_loop(0, 16, write, 0)
    for i in range(16):
        v = gd[i].astype(F32)
        for k in range(16):
            o_gate[4 * i : 4 * i + 4, k * 128 : k * 128 + 128] = v[4 * k : 4 * k + 4]

    last[0].wait_recv()
    for cp in copies.values():
        cp.wait_send()
    for cp in blocks + gates + parts + firsts + rest + last:
        cp.wait_send()

    @pl.when(mine == 0)
    def _():
        for cp in first:
            cp.wait_send()

    @pl.when(sends_far == 1)
    def _():
        to_far.wait_send()

    @pl.when(swaps == 1)
    def _():
        to_near.wait_send()


def on_device(acts, out_grad, saved_proj, weight, shift_scale, gate, image_of):
    n = len(CHUNKS)
    dma = pltpu.SemaphoreType.DMA
    hbm = pl.BlockSpec(memory_space=pl.ANY)
    local = pl.BlockSpec(memory_space=pltpu.VMEM)
    vmem = pltpu.VMEM
    o_acts, o_w, o_mod, o_gate = pl.pallas_call(
        block_kernel,
        out_shape=(
            jax.ShapeDtypeStruct((128, 4096), BF16),
            jax.ShapeDtypeStruct((16, 16, 2048), BF16),
            jax.ShapeDtypeStruct((64, 2, 4096), F32),
            jax.ShapeDtypeStruct((64, 2048), F32),
        ),
        in_specs=[hbm] * 6 + [local],
        out_specs=(local, hbm, local, local),
        scratch_shapes=[
            vmem((128, 4096), BF16), vmem((128, 2048), BF16), vmem((128, 2048), BF16),
            vmem((64, 2048), F32), vmem((64, 2, 4096), F32), vmem((64, 2, 256), F32),
            vmem((128, 128), F32), vmem((8, 128), F32), vmem((16, 128, 2048), BF16),
            vmem((16, 128, 256), BF16), vmem((16, 8, 128), F32), vmem((64, 2048), BF16),
            vmem((16, 64, 128), BF16), vmem((256, 2048), BF16),
            vmem((256, 2048), BF16), vmem((16, 128, 256), F32), vmem((16, 128, 256), F32),
            vmem((16, 128, 256), BF16), vmem((16, 16, 2048), BF16),
            vmem((16, 2, 16, 128), BF16), vmem((16, 16, 2048), BF16),
            vmem((16, 2, 16, 128), BF16), vmem((128, 4096), BF16), vmem((128, 4096), F32),
            vmem((16, 2048), BF16), vmem((2, 16, 128), BF16), vmem((16, 2, 16, 128), BF16),
            vmem((16, 16, 16, 128), BF16), vmem((16, 64, 128), BF16),
            vmem((128, 4096), BF16), vmem((16, 128, 256), BF16),
            dma((n, 7)), dma((n, 7)), dma((n,)), dma((n,)),
            dma((16,)), dma((16,)), dma((16,)), dma((16,)), dma((16,)), dma((16,)),
            dma((2,)), dma,
            dma((16,)), dma((16,)), dma((2, 16)), dma((2, 16)), dma((16,)), dma((16,)),
            dma((15,)), dma((15,)), dma((7,)), dma((7,)), dma((7,)), dma((7,)),
            dma((7,)), dma((7,)), dma((3,)), dma((3,)), dma((7,)),
        ],
        compiler_params=pltpu.CompilerParams(
            collective_id=0, has_side_effects=True, vmem_limit_bytes=52 * 2**20
        ),
        name="adaln_backward",
    )(acts, out_grad, saved_proj, weight, shift_scale, gate, image_of.reshape(1, 128))
    return o_acts, o_w.reshape(256, 2048), o_mod, o_gate


def solution(mesh):
    placed = (
        P(("rep", "shard"), None),
        P(("rep", "shard"), None),
        P(("rep", "shard"), None),
        P("shard", None),
        P(),
        P(),
        P(("rep", "shard")),
    )
    return jax.shard_map(
        on_device,
        mesh=mesh,
        in_specs=placed,
        out_specs=(P(("rep", "shard"), None), P("shard", None), P(), P()),
        check_vma=False,
    )
```

time: 766 us -> 138 us (0.18)
  waiting for transfers between devices: 644 us -> 0 us
  Pallas kernels: 0 us -> 128 us
  blocking collectives: 57.2 us -> 0 us
  matrix products: 32.6 us -> 0 us
  between operations: 13.9 us -> 0.67 us
    psum x2 -> x0, waiting for transfers between devices: 373 us -> none  [the longest x1 264 us: on_device(): lax.psum((mod_part, gate_part), ('rep', 'shard'))]
    all_gather x2 -> x0, waiting for transfers between devices: 270 us -> none  [the longest x1 198 us: on_device(): lax.all_gather(weight, 'shard', axis=0, tiled=True)]
    pallas_call x0 -> x1, Pallas kernels: none -> 128 us  [on_device(): pl.pallas_call(block_kernel, out_shape=(jax.ShapeDtypeStruct((128, 4096),...]
    all_to_all x1 -> x0, blocking collectives: 57.2 us -> none  [on_device(): lax.all_to_all(hidden, 'shard', split_axis=1, concat_axis=0, tiled=True)]
    dot_general x8 -> x0, matrix products: 32.6 us -> none  [the longest x1 14.1 us: on_device(): lax.dot_general(dz, lax.all_gather(weight, 'shard', axis=0, tiled=True),...]
  transfers between devices with their start and end apart: 4 -> 0, of which waited for: 4 -> 0; matrix products, arithmetic and copies ran while one was open for 5% -> 0% of each run, Pallas kernels for 0% -> 0%
where the time goes in v2:
time: 138 us; the launch traced here: 137 us
  Pallas kernels  128 us (93%)
  local copies, waits for them, and re-layouts  8.26 us (6%)
    pallas_call x1, Pallas kernels, on_device(): pl.pallas_call(block_kernel, out_shape=(jax.ShapeDtypeStruct((128, 4096),...  128 us
    unnamed x14, local copies, waits for them, and re-layouts  8.26 us

profile of v2, /device:TPU:1, one launch (start us, length us, event | category | flops | bytes accessed | tf_op | source)
XLA Modules:
  0.0 137.4 jit_solution(1154579958362163026)
XLA Ops:
  0.6 0.0 copy-start
  0.6 1.0 copy-done
  1.7 0.0 copy-start.1
  1.7 1.0 copy-done.1
  2.7 0.0 copy-start.2
  2.7 0.7 copy-done.2
  3.4 128.4 %adaln_backward.1 = (bf16[128,4096]{1,0:T(8,128)(2,1)}, bf16[16,16,2048]{2,1,0:T(8,128)(2,1)}, f32[64,2,4096]{2,1,0:T(2,128)}, f32[64,2048]{1,0:T(8,128)S(1)}) custom-call(bf16[128,4096]{1,0:T(8,128)(2,1)} %acts.1, bf16[128,2048]{1,0:T(8,128)(2,1)S(1)} %copy-done, bf16[128,2048]{1,0:T(8,128)(2,1)S(1)} %copy-done.1, bf16[256,2048]{1,0:T(8,128)(2,1)} %w.1, ...), custom_call_target="tpu_custom_call" | custom-call | tf_op jit(solution)/shard_map/adaln_backward/pallas_call | solution.py:535
  131.8 0.0 copy-start.4
  131.8 0.0 copy-start.3
  131.8 2.4 %copy.15 = bf16[128,4096]{1,0:T(8,128)(2,1)} copy(bf16[128,4096]{1,0:T(8,128)(2,1)} %get-tuple-element.16) | data formatting | bytes 2097152
  134.3 0.0 copy-done.4
  134.3 1.0 copy.16
  135.2 0.0 copy-done.3
  135.2 1.3 copy.17
  136.6 0.8 copy.18
Async XLA Ops:
  0.6 1.0 copy-start
  1.7 1.0 copy-start.1
  2.7 0.7 copy-start.2
  131.8 2.5 %copy-start.4 = (bf16[16,16,2048]{2,1,0:T(8,128)(2,1)S(1)}, bf16[16,16,2048]{2,1,0:T(8,128)(2,1)}, u32[]{:S(2)}) copy-start(bf16[16,16,2048]{2,1,0:T(8,128)(2,1)} %get-tuple-element.9) | copy-start | bytes 3145732
  131.8 3.4 %copy-start.3 = (f32[64,2,4096]{2,1,0:T(2,128)S(1)}, f32[64,2,4096]{2,1,0:T(2,128)}, u32[]{:S(2)}) copy-start(f32[64,2,4096]{2,1,0:T(2,128)} %get-tuple-element.18) | copy-start | bytes 6291460

commit v3 on v2

v3 whole, which is shorter than its diff:
```python
import jax
import jax.numpy as jnp
from jax import lax
from jax.experimental import pallas as pl
from jax.experimental.pallas import tpu as pltpu
from jax.sharding import PartitionSpec as P

MEAN_IMG = 512
MESH = pl.DeviceIdType.MESH
BF16 = jnp.bfloat16
F32 = jnp.float32
CHUNKS = (
    (0, 128, (0, 1, 2)),
    (128, 384, (1, 2, 0)),
    (512, 512, (2, 0, 1)),
    (1024, 128, (0, 1, 2)),
    (1152, 384, (1, 2, 0)),
    (1536, 512, (2, 0, 1)),
)


def signal(at):
    pl.semaphore_signal(
        pltpu.get_barrier_semaphore(), inc=1, device_id=at, device_id_type=MESH
    )


def remote(src, dst, ss, rs, at):
    return pltpu.make_async_remote_copy(
        src_ref=src,
        dst_ref=dst,
        send_sem=ss,
        recv_sem=rs,
        device_id=at,
        device_id_type=MESH,
    )


class Place:
    def __init__(self):
        r, s = lax.axis_index("rep"), lax.axis_index("shard")
        self.r, self.s = r, s
        self.zb, self.x, self.c = lax.div(r, 8), lax.rem(lax.div(r, 2), 4), lax.rem(r, 2)
        self.y, self.zh = lax.div(s, 4), lax.rem(s, 4)
        self.xb, self.yb = lax.rem(self.x, 2), lax.rem(self.y, 2)
        self.xh, self.yh = lax.div(self.x, 2), lax.div(self.y, 2)
        self.odd = lax.rem(self.zh, 2)
        bits = (self.xb, self.yb, self.zb, self.c)
        self.turn = [1 - 2 * b for b in bits]
        self.slot0 = self.xb + 2 * self.yb + 4 * self.zb + 8 * self.c
        p = lax.rem(self.xb + self.c, 2)
        e = lax.rem(self.zb + self.odd, 2)
        self.p, self.e = p, e
        self.e0 = 1 - e
        ys = (self.y, self.y + self.turn[1])
        self.band_y = [[v + w * (3 - 2 * v) for w in (p, 1 - p)] for v in ys]
        self.band_z = []
        for kz in range(2):
            zb, ev = (1 - self.zb, 1 - e) if kz else (self.zb, e)
            row = []
            for kc in range(2):
                c = 1 - self.c if kc else self.c
                row.append(lax.rem(self.zh + c * (2 * zb + 3) + (1 - c) * 2 * (1 - ev), 4))
            self.band_z.append(row)
        self.xs = [lax.rem(self.x + k, 4) for k in range(4)]
        self.ys = [lax.rem(self.y + k, 4) * 4 for k in range(4)]
        self.zs = [lax.rem(self.zh + k, 4) for k in range(4)]

    def mate(self, k):
        r = self.r
        for bit, step in ((0, 2), (2, 8), (3, 1)):
            if k >> bit & 1:
                r = r + step * self.turn[bit]
        return r, self.s + 4 * self.turn[1] if k & 2 else self.s

    def slot(self, k):
        v = self.slot0
        for bit in range(4):
            if k >> bit & 1:
                v = v + (1 << bit) * self.turn[bit]
        return v

    def band(self, k):
        kx, ky, kz, kc = (k >> i & 1 for i in range(4))
        return 4 * self.band_y[ky][kx ^ kc] + self.band_z[kz][kc]

    def far(self):
        z = 2 * self.zh + self.zb + (2 * self.zb - 1) * (3 - 2 * self.c) + 8
        y = self.y + self.p * (3 - 2 * self.y)
        return lax.rem(z, 2) * 8 + self.x * 2 + self.c, y * 4 + lax.rem(lax.div(z, 2), 4)

    def pair(self):
        return self.zb * 8 + (3 - self.x) * 2 + self.c, (3 - self.y) * 4 + self.zh

    def near(self):
        return self.r, (3 - self.y) * 4 + self.zh

    def senders(self):
        found = []
        for k in range(16):
            kx, ky, kz = k % 2, k // 2 % 2, k // 4
            d = (4 - kz) % 4
            c = d % 2
            if c:
                zb = (3 - d) // 2
            else:
                zb = 1 - self.odd if (1 + d // 2 + kz) % 2 else self.odd
            xh = 1 - self.xh if kx else self.xh
            y = 3 - self.y if ky else self.y
            found.append((zb * 8 + (2 * xh + (ky + c) % 2) * 2 + c, y * 4 + self.zs[kz]))
        return found

    def holders(self, band):
        zs, cs = (self.zb, 1 - self.zb), (self.c, 1 - self.c)
        return [
            (
                2 * self.xs[k % 4] + zs[k // 4 % 2] + 8 * cs[k // 8],
                (zs[k // 4 % 2] * 8 + self.xs[k % 4] * 2 + cs[k // 8], band),
            )
            for k in range(16)
        ]

    def near_holders(self, band):
        far = 1 - (1 - self.c) * self.e
        zb = self.zb + self.turn[2] * far
        cs = (self.c, 1 - self.c)
        return [
            (
                2 * self.xs[k % 4] + 8 * cs[k // 4],
                (zb * 8 + self.xs[k % 4] * 2 + cs[k // 4], band),
            )
            for k in range(8)
        ]

    def plane(self):
        return [(self.r, self.ys[k // 4] + self.zs[k % 4]) for k in range(1, 16)]

    def line(self):
        zs = (self.zb, 1 - self.zb)
        return [(zs[k // 4] * 8 + self.xs[k % 4] * 2 + self.c, self.s) for k in range(1, 8)]


def dot(a, b, dims):
    return lax.dot_general(a, b, (dims, ((), ())), preferred_element_type=F32)


def two_terms(v):
    hi = v.astype(BF16)
    return hi, (v - hi.astype(F32)).astype(BF16)


def image_hot(ids, count):
    rows = lax.broadcasted_iota(jnp.int32, (count, ids.shape[1]), 0).astype(F32)
    return jnp.where(rows == ids, 1.0, 0.0)


def block_kernel(
    acts, og, sp, w, ss, gate, ids,
    o_acts, o_w, o_mod, o_gate,
    acts_v, og_v, sp_v, gate_v, ss_v, ss_b, rm, st, dz_all, acts_b, st_b,
    gm, gm_o, gm_i, gm_t, gm_b, w_b, hid, nrm, dh, dh_b, msg_a, msg_b, msg_s, part_a, part_b, part_s,
    dh_full, sc1, wp, s_own, s1, rec, o2, v2, acc, to_z, from_z, at_z,
    dz_s, dz_r, core_s, core_r, ac_s, ac_r, st_s, st_r, gm_s, gm_r, w_s, w_r,
    dh_s, dh_r, mw_s, mw_r, ms_s, ms_r, s1_s, s1_r, wp_s, wp_r, sm_s, sm_r, co_s, co_r, tz_s, tz_r, loc,
):
    me = Place()
    c, g, b = me.c, me.slot0, me.band(0)
    far, near = me.far(), me.near()
    keeps = (1 - c) * me.e * (1 - me.p)
    swaps = (1 - c) * me.e * me.p
    takes_half = (1 - c) * (1 - me.e)
    pair = me.pair()
    mine = keeps
    q = me.xh + 2 * me.yh + 4 * me.zh
    h = 2 * me.x + me.zb + 8 * c
    kept = me.s
    sib = me.mate(8)
    plane, line = me.plane(), me.line()
    cz = 2 * c + me.zb
    octet = g - 8 * c
    band_cols = pl.ds(pl.multiple_of(b * 256, 256), 256)

    def own_core(bits, at, width):
        return dz_all.at[
            pl.ds(2 * c, 2) if bits & 4 else cz,
            pl.ds(0, 2) if bits & 2 else me.yb,
            pl.ds(0, 2) if bits & 1 else me.xb,
            :,
            pl.ds(at, width),
        ]

    loads = [
        pltpu.make_async_copy(a, v, loc.at[i])
        for i, (a, v) in enumerate(
            ((og, og_v), (gate, gate_v), (acts, acts_v), (sp, sp_v),
             (ss.at[:, :, band_cols], ss_b), (ss, ss_v), (acts.at[:, band_cols], acts_b.at[g]))
        )
    ]
    for cp in loads:
        cp.start()
    for k in range(1, 16):
        signal(me.mate(k))
    signal(far)

    @pl.when(swaps == 1)
    def _():
        signal(near)

    @pl.when(takes_half == 1)
    def _():
        signal(pair)

    senders = me.senders()

    @pl.when(mine == 0)
    def _():
        signal(senders[0])

    for to in senders[1:]:
        signal(to)
    for to in plane + line:
        signal(to)

    ids_f = ids[...].astype(F32)
    hot = image_hot(ids_f, 128)
    hot_t = hot.T[:, :64].astype(BF16)
    loads[0].wait()
    loads[1].wait()
    for j in range(0, 2048, 512):
        cols = slice(j, j + 512)
        hi, lo = two_terms(gate_v[:, cols])
        rows = dot(hot_t, hi, ((1,), (0,))) + dot(hot_t, lo, ((1,), (0,)))
        dz_all[cz, me.yb, me.xb, :, cols] = (rows * og_v[:, cols].astype(F32)).astype(BF16)

    pl.semaphore_wait(pltpu.get_barrier_semaphore(), 54 + swaps + takes_half - mine)

    copies = {}

    def stage(k, half):
        for n in range(3 * half, 3 * half + 3):
            at, width, order = CHUNKS[n]
            if k:
                copies[n, k - 1].wait_recv()
            slots = own_core(sum(1 << d for d in order[:k]), at, width)
            cp = remote(slots, slots, dz_s.at[n, k], dz_r.at[n, k], me.mate(1 << order[k]))
            cp.start()
            copies[n, k] = cp

    stage(0, 0)

    half_rows = pl.ds(pl.multiple_of(128 * lax.div(me.x, 2), 128), 128)
    to_far = remote(w, w_b, w_s.at[0], w_r.at[0], far)
    to_near = remote(w, w_b, w_s.at[1], w_r.at[0], near)
    to_self = pltpu.make_async_copy(w, w_b, w_r.at[0])
    half_far = remote(w.at[half_rows], w_b.at[half_rows], w_s.at[2], w_r.at[1], far)
    half_twin = remote(w_b.at[half_rows], w_b.at[half_rows], w_s.at[3], w_r.at[2], pair)

    @pl.when(c == 1)
    def _():
        to_far.start()

    @pl.when((1 - c) * me.e == 1)
    def _():
        half_far.start()

    @pl.when(swaps == 1)
    def _():
        to_near.start()

    @pl.when(keeps == 1)
    def _():
        to_self.start()

    loads[2].wait()

    def stats(i, _):
        rows = pl.ds(pl.multiple_of(i * 16, 16), 16)
        v = acts_v[rows, :].astype(F32)
        m = jnp.mean(v, axis=1, keepdims=True)
        v = v - m
        r = lax.rsqrt(jnp.mean(v * v, axis=1, keepdims=True) + 1e-06)
        lane = lax.broadcasted_iota(jnp.int32, (16, 128), 1)
        rm[rows, :] = jnp.where(lane == 0, r, jnp.where(lane == 1, m, 0.0))
        return 0

    lax.fori_loop(0, 8, stats, 0)
    turned = rm[...].T[:8, :]
    row = lax.broadcasted_iota(jnp.int32, (8, 128), 0)
    st[...] = jnp.where(row == 2, ids_f, turned)
    st_b[g] = st[...]

    stage(1, 0)
    stage(0, 1)

    blocks = []
    for k in range(1, 16):
        cols = pl.ds(pl.multiple_of(me.band(k) * 256, 256), 256)
        cp = remote(acts.at[:, cols], acts_b.at[g], ac_s.at[k], ac_r.at[k], me.mate(k))
        cp.start()
        blocks.append(cp)

    for k in range(1, 16):
        cp = remote(st, st_b.at[g], st_s.at[k], st_r.at[k], me.mate(k))
        cp.start()
        blocks.append(cp)

    loads[3].wait()
    hot_b = hot[:64].astype(BF16)
    for j in range(0, 2048, 512):
        cols = slice(j, j + 512)
        hi, lo = two_terms(og_v[:, cols].astype(F32) * sp_v[:, cols].astype(F32))
        gm[:, cols] = (dot(hot_b, hi, ((1,), (0,))) + dot(hot_b, lo, ((1,), (0,)))).astype(BF16)
    for k in range(16):
        gm_o[me.slot(k)] = gm[:, pl.ds(pl.multiple_of(me.band(k) * 128, 128), 128)]
    swap = remote(gm_o.at[pl.ds(8 - 8 * c, 8)], gm_i, gm_s.at[0], gm_r.at[0], sib)
    swap.start()

    stage(2, 0)
    stage(1, 1)

    @pl.when(takes_half == 1)
    def _():
        half_far.wait_recv()
        half_twin.start()

    stage(2, 1)

    loads[5].wait()

    def scales(j, _):
        cols = pl.ds(pl.multiple_of(j * 512, 512), 512)
        hi, lo = two_terms(ss_v[:, 1, cols])
        sc1[:, cols] = 1.0 + (dot(hot_t, hi, ((1,), (0,))) + dot(hot_t, lo, ((1,), (0,))))
        return 0

    lax.fori_loop(0, 8, scales, 0)

    loads[4].wait()
    loads[6].wait()
    for cp in blocks:
        cp.wait_recv()
    shift_hi, shift_lo = two_terms(ss_b[:, 0, :])
    scale_hi, scale_lo = two_terms(ss_b[:, 1, :])
    tables = jnp.concatenate(
        [
            jnp.concatenate([shift_hi, scale_hi], axis=1),
            jnp.concatenate([shift_lo, scale_lo], axis=1),
        ],
        axis=0,
    )

    def modulate(t, _):
        block = st_b[t]
        wide = jnp.concatenate([block, jnp.zeros((120, 128), F32)], axis=0).T
        r, m = wide[:, 0:1], wide[:, 1:2]
        own = image_hot(block[2:3], 64)
        twice = jnp.concatenate([own, own], axis=0).T.astype(BF16)
        mods = dot(twice, tables, ((1,), (0,)))
        normed = (acts_b[t].astype(F32) - m) * r
        nrm[t] = normed
        out = normed * (1.0 + mods[:, 256:]) + mods[:, :256]
        hid[:, pl.ds(pl.multiple_of(t * 128, 128), 128)] = out.T.astype(BF16)
        rows = lax.broadcasted_iota(jnp.int32, (128, 128), 0)
        hit = ((rows // 2).astype(F32) == block[2:3])
        o2[:, pl.ds(pl.multiple_of(t * 128, 128), 128)] = jnp.where(
            hit & (rows % 2 == 0), 1.0, 0.0
        ).astype(BF16)
        o2[:, pl.ds(pl.multiple_of(2048 + t * 128, 128), 128)] = jnp.where(
            hit & (rows % 2 == 1), 1.0, 0.0
        ).astype(BF16)
        return 0

    lax.fori_loop(0, 16, modulate, 0)

    swap.wait_recv()
    gm_t[...] = (gm_o[pl.ds(8 * c, 8)].astype(F32) + gm_i[...].astype(F32)).astype(BF16)
    gm_b[octet] = gm_t[octet]
    gates = []
    for k in range(1, 8):
        cp = remote(
            gm_t.at[me.slot(k) - 8 * c], gm_b.at[octet], gm_s.at[k], gm_r.at[k], me.mate(k)
        )
        cp.start()
        gates.append(cp)

    parts, first = [], []

    def arrive(half):
        for n in range(3 * half, 3 * half + 3):
            at, width, _ = CHUNKS[n]
            copies[n, 2].wait_recv()
            slots = own_core(7, at, width)
            cp = remote(slots, slots, core_s.at[n], core_r.at[n], sib)
            cp.start()
            copies[n, 3] = cp

    def complete(half):
        for n in range(3 * half, 3 * half + 3):
            copies[n, 3].wait_recv()

    def give(pieces, into, ss_, rs_):
        for k, (piece, to) in enumerate(pieces):
            cp = remote(piece, into, ss_.at[k], rs_.at[q], to)
            if k == 0:
                keep = pltpu.make_async_copy(piece, into, rs_.at[q])
                first.append(cp)

                @pl.when(mine == 0)
                def _():
                    cp.start()

                @pl.when(mine == 1)
                def _():
                    keep.start()

            else:
                cp.start()
                parts.append(cp)

    def give_rows(msg, part, half):
        pieces = [(msg.at[pl.ds(i, 2)], to) for i, to in me.near_holders(b)]
        give(pieces, part.at[q], mw_s.at[half], mw_r.at[half])

    def weight_grad(msg, half):
        def grads(j, _):
            cols = pl.ds(pl.multiple_of(half * 1024 + j * 256, 256), 256)
            v = dot(hid[...], dz_all[:, :, :, :, cols].reshape(2048, 256), ((1,), (0,)))
            cols = pl.ds(pl.multiple_of(j * 256, 256), 256)
            msg[:, :, cols] = v.astype(BF16).reshape(16, 16, 256)
            return 0

        lax.fori_loop(0, 4, grads, 0)

    def back(half):
        def some(t, _):
            rows = pl.ds(t * 4, 4)
            v = dot(
                dz_all[t, :, :, :, half * 1024 : half * 1024 + 1024].reshape(512, 1024),
                w_b[:, half * 1024 : half * 1024 + 1024],
                ((1,), (1,)),
            ).reshape(4, 128, 256)
            if half == 0:
                dh[rows] = v
            else:
                v = v + dh[rows]
                dh_b[rows] = v.astype(BF16)
                v2[rows] = (v * nrm[rows]).astype(BF16)
            return 0

        lax.fori_loop(0, 4, some, 0)

    arrive(0)
    complete(0)
    weight_grad(msg_a, 0)
    give_rows(msg_a, part_a, 0)
    arrive(1)

    @pl.when(takes_half == 1)
    def _():
        half_twin.wait_recv()

    @pl.when(takes_half == 0)
    def _():
        to_far.wait_recv()

    back(0)
    for cp in gates[:7]:
        cp.wait_recv()
    gate_sum = gm_b[0].astype(F32)
    for t in range(1, 8):
        gate_sum = gate_sum + gm_b[t].astype(F32)
    at_row = lax.broadcasted_iota(jnp.int32, (256, 64), 0)
    image = lax.broadcasted_iota(jnp.int32, (256, 64), 1)
    put = (at_row % 16 < 4) & (image == at_row // 16 * 4 + at_row % 16)
    spaced = dot(
        jnp.where(put, 1.0, 0.0).astype(BF16), gate_sum.astype(BF16), ((1,), (0,))
    ).astype(BF16)
    msg_s[:, 1] = spaced.reshape(16, 16, 128)
    complete(1)
    back(1)

    sums = dot(o2[:, :2048], dh_b[...].reshape(2048, 256), ((1,), (0,)))
    sums = sums + dot(o2[:, 2048:], v2[...].reshape(2048, 256), ((1,), (0,)))
    for i in range(16):
        rows = slice(8 * i, 8 * i + 8)
        both = jnp.concatenate([sums[rows, :128], sums[rows, 128:]], axis=0)
        msg_s[i, 0] = both.astype(BF16)


    give([(msg_s.at[i], to) for i, to in me.holders(b)], part_s.at[q], ms_s, ms_r)
    dh_full[:, band_cols] = dh_b[g]
    for k in range(1, 16):
        cp = remote(
            dh_b.at[me.slot(k)], dh_full.at[:, band_cols], dh_s.at[k], dh_r.at[k], me.mate(k)
        )
        cp.start()
        gates.append(cp)
    weight_grad(msg_b, 1)
    give_rows(msg_b, part_b, 1)

    comes = (1 - me.e0, me.zb, 1 - me.e0, 1 - me.zb)

    def collect(part, half):
        acc[...] = jnp.zeros_like(acc)
        for kz in range(4):

            @pl.when(comes[kz] == 1)
            def _():
                for k in range(4):
                    at = 4 * me.zs[kz] + k
                    pltpu.make_async_copy(part.at[at], part.at[at], mw_r.at[half, at]).wait()
                total = part[4 * me.zs[kz]].astype(F32)
                for k in range(1, 4):
                    total = total + part[4 * me.zs[kz] + k].astype(F32)
                acc[...] += total

        to_z[half] = acc[1 - me.zb].astype(BF16)
        at_z[half] = acc[me.zb]
        cp = remote(to_z.at[half], from_z.at[half], tz_s.at[half], tz_r.at[half], me.mate(4))
        cp.start()
        return cp

    for k in range(16):
        pltpu.make_async_copy(part_s.at[k], part_s.at[k], ms_r.at[k]).wait()
    total = part_s[0].astype(F32)
    for k in range(1, 16):
        total = total + part_s[k].astype(F32)
    s_own[...] = (total * MEAN_IMG ** (-0.5)).astype(BF16)
    s1[kept] = s_own[...]
    firsts = []
    for k, to in enumerate(plane):
        cp = remote(s_own, s1.at[kept], s1_s.at[k], s1_r.at[k], to)
        cp.start()
        firsts.append(cp)

    def finish(i, _):
        rows = pl.ds(pl.multiple_of(i * 16, 16), 16)
        r, m = rm[rows, 0:1], rm[rows, 1:2]
        normed = (acts_v[rows, :].astype(F32) - m) * r
        dn = dh_full[rows, :].astype(F32) * sc1[rows, :]
        mean = jnp.mean(dn, axis=1, keepdims=True)
        along = jnp.mean(dn * normed, axis=1, keepdims=True)
        o_acts[rows, :] = (r * (dn - mean - normed * along)).astype(BF16)
        return 0

    zed = [collect(part_a, 0)]
    rest = []
    for cp in firsts:
        cp.wait_recv()
    rec[h, :16] = s1[:, 0]
    rec[h, 16:] = (
        jnp.concatenate([s1[k, 1].astype(F32)[:4] for k in range(16)], axis=0)
        .astype(BF16)
        .reshape(4, 16, 128)
    )
    for k, to in enumerate(line):
        cp = remote(rec.at[h], rec.at[h], sm_s.at[k], sm_r.at[k], to)
        cp.start()
        rest.append(cp)
    zed.append(collect(part_b, 1))
    for half in range(2):
        zed[half].wait_recv()
        total = at_z[half] + from_z[half].astype(F32)
        cols = slice(half * 1024, half * 1024 + 1024)
        wp[:, cols] = (total * 32768 ** (-0.5)).astype(BF16)
    own_w = pltpu.make_async_copy(wp, o_w.at[h], loc.at[0])
    own_w.start()
    for k, to in enumerate(line):
        cp = remote(wp, o_w.at[h], wp_s.at[k], wp_r.at[k], to)
        cp.start()
        rest.append(cp)

    for cp in gates[7:]:
        cp.wait_recv()

    lax.fori_loop(0, 8, finish, 0)

    own_w.wait()
    mates = pl.ds(c * 8, 8)
    last = []
    for i, v in ((0, rec), (1, o_w)):
        for cp in rest[7 * i : 7 * i + 7]:
            cp.wait_recv()
        cp = remote(v.at[mates], v.at[mates], co_s.at[i], co_r.at[i], sib)
        cp.start()
        last.append(cp)
    last[0].wait_recv()

    def write(i, _):
        images = pl.ds(i * 4, 4)
        for k in range(16):
            v = rec[i, k].astype(F32)
            o_mod[images, :, k * 256 : k * 256 + 128] = v[:8].reshape(4, 2, 128)
            o_mod[images, :, k * 256 + 128 : k * 256 + 256] = v[8:].reshape(4, 2, 128)
        return 0

    lax.fori_loop(0, 16, write, 0)
    for i in range(16):
        v = rec[i, 16:].reshape(64, 128).astype(F32)
        for k in range(16):
            o_gate[4 * i : 4 * i + 4, k * 128 : k * 128 + 128] = v[4 * k : 4 * k + 4]

    last[1].wait_recv()
    for cp in copies.values():
        cp.wait_send()
    for cp in blocks + [swap] + gates + parts + firsts + rest + last + zed:
        cp.wait_send()

    @pl.when(mine == 0)
    def _():
        for cp in first:
            cp.wait_send()

    @pl.when(c == 1)
    def _():
        to_far.wait_send()

    @pl.when((1 - c) * me.e == 1)
    def _():
        half_far.wait_send()

    @pl.when(takes_half == 1)
    def _():
        half_twin.wait_send()

    @pl.when(swaps == 1)
    def _():
        to_near.wait_send()


def on_device(acts, out_grad, saved_proj, weight, shift_scale, gate, image_of):
    n = len(CHUNKS)
    dma = pltpu.SemaphoreType.DMA
    hbm = pl.BlockSpec(memory_space=pl.ANY)
    local = pl.BlockSpec(memory_space=pltpu.VMEM)
    vmem = pltpu.VMEM
    o_acts, o_w, o_mod, o_gate = pl.pallas_call(
        block_kernel,
        out_shape=(
            jax.ShapeDtypeStruct((128, 4096), BF16),
            jax.ShapeDtypeStruct((16, 16, 2048), BF16),
            jax.ShapeDtypeStruct((64, 2, 4096), F32),
            jax.ShapeDtypeStruct((64, 2048), F32),
        ),
        in_specs=[pl.BlockSpec(memory_space=pltpu.HBM)] * 6 + [local],
        out_specs=(local, hbm, local, local),
        scratch_shapes=[
            vmem((128, 4096), BF16), vmem((128, 2048), BF16), vmem((128, 2048), BF16),
            vmem((64, 2048), F32), vmem((64, 2, 4096), F32), vmem((64, 2, 256), F32),
            vmem((128, 128), F32), vmem((8, 128), F32), vmem((4, 2, 2, 128, 2048), BF16),
            vmem((16, 128, 256), BF16), vmem((16, 8, 128), F32),
            vmem((64, 2048), BF16), vmem((16, 64, 128), BF16), vmem((8, 64, 128), BF16),
            vmem((8, 64, 128), BF16), vmem((8, 64, 128), BF16), vmem((256, 2048), BF16),
            vmem((256, 2048), BF16), vmem((16, 128, 256), F32), vmem((16, 128, 256), F32),
            vmem((16, 128, 256), BF16), vmem((16, 16, 1024), BF16), vmem((16, 16, 1024), BF16),
            vmem((16, 2, 16, 128), BF16), vmem((16, 2, 16, 1024), BF16),
            vmem((16, 2, 16, 1024), BF16), vmem((16, 2, 16, 128), BF16),
            vmem((128, 4096), BF16), vmem((128, 4096), F32), vmem((16, 2048), BF16),
            vmem((2, 16, 128), BF16), vmem((16, 2, 16, 128), BF16),
            vmem((16, 20, 16, 128), BF16), vmem((128, 4096), BF16), vmem((16, 128, 256), BF16),
            vmem((2, 16, 1024), F32), vmem((2, 16, 1024), BF16), vmem((2, 16, 1024), BF16),
            vmem((2, 16, 1024), F32),
            dma((n, 3)), dma((n, 3)), dma((n,)), dma((n,)),
            dma((16,)), dma((16,)), dma((16,)), dma((16,)), dma((8,)), dma((8,)),
            dma((4,)), dma((3,)), dma((16,)), dma((16,)), dma((2, 8)), dma((2, 16)),
            dma((16,)), dma((16,)), dma((15,)), dma((15,)), dma((7,)), dma((7,)), dma((7,)), dma((7,)),
            dma((2,)), dma((2,)), dma((2,)), dma((2,)), dma((7,)),
        ],
        compiler_params=pltpu.CompilerParams(
            collective_id=0, has_side_effects=True, vmem_limit_bytes=60 * 2**20
        ),
        name="adaln_backward",
    )(acts, out_grad, saved_proj, weight, shift_scale, gate, image_of.reshape(1, 128))
    return o_acts, o_w.reshape(256, 2048), o_mod, o_gate


def solution(mesh):
    placed = (
        P(("rep", "shard"), None),
        P(("rep", "shard"), None),
        P(("rep", "shard"), None),
        P("shard", None),
        P(),
        P(),
        P(("rep", "shard")),
    )
    return jax.shard_map(
        on_device,
        mesh=mesh,
        in_specs=placed,
        out_specs=(P(("rep", "shard"), None), P("shard", None), P(), P()),
        check_vma=False,
    )
```

time: 138 us -> 133 us (0.964)
  local copies, waits for them, and re-layouts: 8.26 us -> 5.61 us
    unnamed x14 -> x10, local copies, waits for them, and re-layouts: 8.26 us -> 5.61 us
    pallas_call x1, Pallas kernels: 128 us -> 127 us  [on_device(): pl.pallas_call(block_kernel, out_shape=(jax.ShapeDtypeStruct((128, 4096),...]
where the time goes in v3:
time: 133 us
  Pallas kernels  127 us (95%)
  local copies, waits for them, and re-layouts  5.61 us (4%)
    pallas_call x1, Pallas kernels, on_device(): pl.pallas_call(block_kernel, out_shape=(jax.ShapeDtypeStruct((128, 4096),...  127 us
    unnamed x10, local copies, waits for them, and re-layouts  5.61 us

profile of v3, /device:TPU:1, one launch (start us, length us, event | category | flops | bytes accessed | tf_op | source)
XLA Modules:
  0.0 132.9 jit_solution(13487194662482641218)
XLA Ops:
  0.6 126.6 %adaln_backward.1 = (bf16[128,4096]{1,0:T(8,128)(2,1)}, bf16[16,16,2048]{2,1,0:T(8,128)(2,1)}, f32[64,2,4096]{2,1,0:T(2,128)}, f32[64,2048]{1,0:T(8,128)}) custom-call(bf16[128,4096]{1,0:T(8,128)(2,1)} %acts.1, bf16[128,2048]{1,0:T(8,128)(2,1)} %og.1, bf16[128,2048]{1,0:T(8,128)(2,1)} %sp.1, bf16[256,2048]{1,0:T(8,128)(2,1)} %w.1, f32[64,2,4096]{2,1,0:T(2,128)} %ss.1, ...), custom_call_target="tpu_custom_call" | custom-call | tf_op jit(solution)/shard_map/adaln_backward/pallas_call | solution.py:637
  127.2 0.0 copy-start.1
  127.2 0.0 copy-start
  127.2 2.4 %copy.15 = bf16[128,4096]{1,0:T(8,128)(2,1)} copy(bf16[128,4096]{1,0:T(8,128)(2,1)} %get-tuple-element.16) | data formatting | bytes 2097152
  129.7 0.0 copy-done.1
  129.7 1.0 copy.16
  130.7 0.0 copy-done
  130.7 0.0 copy-start.2
  130.7 1.3 copy.17
  132.0 0.1 copy-done.2
  132.1 0.8 copy.18
Async XLA Ops:
  127.2 2.5 %copy-start.1 = (bf16[16,16,2048]{2,1,0:T(8,128)(2,1)S(1)}, bf16[16,16,2048]{2,1,0:T(8,128)(2,1)}, u32[]{:S(2)}) copy-start(bf16[16,16,2048]{2,1,0:T(8,128)(2,1)} %get-tuple-element.9) | copy-start | bytes 3145732
  127.2 3.4 %copy-start = (f32[64,2,4096]{2,1,0:T(2,128)S(1)}, f32[64,2,4096]{2,1,0:T(2,128)}, u32[]{:S(2)}) copy-start(f32[64,2,4096]{2,1,0:T(2,128)} %get-tuple-element.18) | copy-start | bytes 6291460
  130.7 1.4 %copy-start.2 = (f32[64,2048]{1,0:T(8,128)S(1)}, f32[64,2048]{1,0:T(8,128)}, u32[]{:S(2)}) copy-start(f32[64,2048]{1,0:T(8,128)} %get-tuple-element.19) | copy-start | bytes 1572868

commit v4 on v3

--- a/solution.py
+++ b/solution.py
@@ -11,12 +11,14 @@
 F32 = jnp.float32
 CHUNKS = (
     (0, 128, (0, 1, 2)),
-    (128, 384, (1, 2, 0)),
-    (512, 512, (2, 0, 1)),
-    (1024, 128, (0, 1, 2)),
-    (1152, 384, (1, 2, 0)),
+    (128, 256, (1, 2, 0)),
+    (384, 384, (2, 0, 1)),
+    (768, 256, (0, 1, 2)),
+    (1024, 512, (1, 2, 0)),
     (1536, 512, (2, 0, 1)),
 )
+SPLIT = 768
+WIDE = (768, 1280)
 
 
 def signal(at):
@@ -156,10 +158,10 @@
 
 def block_kernel(
     acts, og, sp, w, ss, gate, ids,
-    o_acts, o_w, o_mod, o_gate,
+    o_acts, o_w, o_rec,
     acts_v, og_v, sp_v, gate_v, ss_v, ss_b, rm, st, dz_all, acts_b, st_b,
     gm, gm_o, gm_i, gm_t, gm_b, w_b, hid, nrm, dh, dh_b, msg_a, msg_b, msg_s, part_a, part_b, part_s,
-    dh_full, sc1, wp, s_own, s1, rec, o2, v2, acc, to_z, from_z, at_z,
+    dh_full, sc1, wp, s_own, s1, rec, ga, o2, v2, acc, to_z, from_z, at_z,
     dz_s, dz_r, core_s, core_r, ac_s, ac_r, st_s, st_r, gm_s, gm_r, w_s, w_r,
     dh_s, dh_r, mw_s, mw_r, ms_s, ms_r, s1_s, s1_r, wp_s, wp_r, sm_s, sm_r, co_s, co_r, tz_s, tz_r, loc,
 ):
@@ -423,20 +425,22 @@
 
     def weight_grad(msg, half):
         def grads(j, _):
-            cols = pl.ds(pl.multiple_of(half * 1024 + j * 256, 256), 256)
+            cols = pl.ds(pl.multiple_of(half * SPLIT + j * 256, 256), 256)
             v = dot(hid[...], dz_all[:, :, :, :, cols].reshape(2048, 256), ((1,), (0,)))
             cols = pl.ds(pl.multiple_of(j * 256, 256), 256)
             msg[:, :, cols] = v.astype(BF16).reshape(16, 16, 256)
             return 0
 
-        lax.fori_loop(0, 4, grads, 0)
+        lax.fori_loop(0, WIDE[half] // 256, grads, 0)
 
     def back(half):
+        lo, hi = half * SPLIT, half * SPLIT + WIDE[half]
+
         def some(t, _):
             rows = pl.ds(t * 4, 4)
             v = dot(
-                dz_all[t, :, :, :, half * 1024 : half * 1024 + 1024].reshape(512, 1024),
-                w_b[:, half * 1024 : half * 1024 + 1024],
+                dz_all[t, :, :, :, lo:hi].reshape(512, hi - lo),
+                w_b[:, lo:hi],
                 ((1,), (1,)),
             ).reshape(4, 128, 256)
             if half == 0:
@@ -501,6 +505,7 @@
     comes = (1 - me.e0, me.zb, 1 - me.e0, 1 - me.zb)
 
     def collect(part, half):
+        wide = WIDE[half]
         acc[...] = jnp.zeros_like(acc)
         for kz in range(4):
 
@@ -512,11 +517,13 @@
                 total = part[4 * me.zs[kz]].astype(F32)
                 for k in range(1, 4):
                     total = total + part[4 * me.zs[kz] + k].astype(F32)
-                acc[...] += total
+                acc[:, :, :wide] += total
 
         to_z[half] = acc[1 - me.zb].astype(BF16)
         at_z[half] = acc[me.zb]
-        cp = remote(to_z.at[half], from_z.at[half], tz_s.at[half], tz_r.at[half], me.mate(4))
+        cp = remote(
+            to_z.at[half, :, pl.ds(0, wide)], from_z.at[half, :, pl.ds(0, wide)], tz_s.at[half], tz_r.at[half], me.mate(4),
+        )
         cp.start()
         return cp
 
@@ -540,92 +547,128 @@
         dn = dh_full[rows, :].astype(F32) * sc1[rows, :]
         mean = jnp.mean(dn, axis=1, keepdims=True)
         along = jnp.mean(dn * normed, axis=1, keepdims=True)
-        o_acts[rows, :] = (r * (dn - mean - normed * along)).astype(BF16)
+        ga[rows, :] = (r * (dn - mean - normed * along)).astype(BF16)
         return 0
 
     zed = [collect(part_a, 0)]
-    rest = []
+    rest, own_w, w_line = [], [], []
+
+    def send_rows(half):
+        zed[half].wait_recv()
+        total = at_z[half] + from_z[half].astype(F32)
+        cols = slice(half * SPLIT, half * SPLIT + WIDE[half])
+        wp[:, cols] = (total[:, : WIDE[half]] * 32768 ** (-0.5)).astype(BF16)
+        piece, into = wp.at[:, cols], o_w.at[h, :, cols]
+        own_w.append(pltpu.make_async_copy(piece, into, loc.at[3 + half]))
+        own_w[half].start()
+        for k, to in enumerate(line):
+            cp = remote(piece, into, wp_s.at[half, k], wp_r.at[half, k], to)
+            cp.start()
+            w_line.append(cp)
+
+    send_rows(0)
     for cp in firsts:
         cp.wait_recv()
-    rec[h, :16] = s1[:, 0]
-    rec[h, 16:] = (
+    rec[:16] = s1[:, 0]
+    rec[16:] = (
         jnp.concatenate([s1[k, 1].astype(F32)[:4] for k in range(16)], axis=0)
         .astype(BF16)
         .reshape(4, 16, 128)
     )
+    own_rec = pltpu.make_async_copy(rec, o_rec.at[h], loc.at[1])
+    own_rec.start()
     for k, to in enumerate(line):
-        cp = remote(rec.at[h], rec.at[h], sm_s.at[k], sm_r.at[k], to)
+        cp = remote(rec, o_rec.at[h], sm_s.at[k], sm_r.at[k], to)
         cp.start()
         rest.append(cp)
     zed.append(collect(part_b, 1))
-    for half in range(2):
-        zed[half].wait_recv()
-        total = at_z[half] + from_z[half].astype(F32)
-        cols = slice(half * 1024, half * 1024 + 1024)
-        wp[:, cols] = (total * 32768 ** (-0.5)).astype(BF16)
-    own_w = pltpu.make_async_copy(wp, o_w.at[h], loc.at[0])
-    own_w.start()
-    for k, to in enumerate(line):
-        cp = remote(wp, o_w.at[h], wp_s.at[k], wp_r.at[k], to)
-        cp.start()
-        rest.append(cp)
-
+    send_rows(1)
     for cp in gates[7:]:
         cp.wait_recv()
 
     lax.fori_loop(0, 8, finish, 0)
-
-    own_w.wait()
+    out = pltpu.make_async_copy(ga, o_acts, loc.at[2])
+    out.start()
+
     mates = pl.ds(c * 8, 8)
     last = []
-    for i, v in ((0, rec), (1, o_w)):
-        for cp in rest[7 * i : 7 * i + 7]:
+    own_rec.wait()
+    for cp in own_w:
+        cp.wait()
+    for i, (v, sent) in enumerate(((o_rec, rest), (o_w, w_line))):
+        for cp in sent:
             cp.wait_recv()
         cp = remote(v.at[mates], v.at[mates], co_s.at[i], co_r.at[i], sib)
         cp.start()
         last.append(cp)
     last[0].wait_recv()
+    last[1].wait_recv()
+    out.wait()
+    for cp in copies.values():
+        cp.wait_send()
+    for cp in blocks + [swap] + gates + parts + firsts + rest + w_line + last + zed:
+        cp.wait_send()
+
+    @pl.when(mine == 0)
+    def _():
+        for cp in first:
+            cp.wait_send()
+
+    @pl.when(c == 1)
+    def _():
+        to_far.wait_send()
+
+    @pl.when((1 - c) * me.e == 1)
+    def _():
+        half_far.wait_send()
+
+    @pl.when(takes_half == 1)
+    def _():
+        half_twin.wait_send()
+
+    @pl.when(swaps == 1)
+    def _():
+        to_near.wait_send()
+
+
+def lay_out_kernel(acts, w, rec_in, o_acts, o_w, o_mod, o_gate, rec, mod, gate, va, vw, sem):
+    fetch = [
+        pltpu.make_async_copy(a, v, sem.at[i])
+        for i, (a, v) in enumerate(((rec_in, rec), (acts, va), (w, vw)))
+    ]
+    for cp in fetch:
+        cp.start()
+    fetch[0].wait()
+    sent = []
 
     def write(i, _):
         images = pl.ds(i * 4, 4)
         for k in range(16):
             v = rec[i, k].astype(F32)
-            o_mod[images, :, k * 256 : k * 256 + 128] = v[:8].reshape(4, 2, 128)
-            o_mod[images, :, k * 256 + 128 : k * 256 + 256] = v[8:].reshape(4, 2, 128)
+            mod[images, :, k * 256 : k * 256 + 128] = v[:8].reshape(4, 2, 128)
+            mod[images, :, k * 256 + 128 : k * 256 + 256] = v[8:].reshape(4, 2, 128)
         return 0
 
-    lax.fori_loop(0, 16, write, 0)
+    for half in range(2):
+        lax.fori_loop(8 * half, 8 * half + 8, write, 0)
+        images = pl.ds(32 * half, 32)
+        cp = pltpu.make_async_copy(mod.at[images], o_mod.at[images], sem.at[3 + half])
+        cp.start()
+        sent.append(cp)
+        fetch[1 + half].wait()
+        v, o = ((va, o_acts), (vw, o_w))[half]
+        cp = pltpu.make_async_copy(v, o, sem.at[5 + half])
+        cp.start()
+        sent.append(cp)
     for i in range(16):
         v = rec[i, 16:].reshape(64, 128).astype(F32)
         for k in range(16):
-            o_gate[4 * i : 4 * i + 4, k * 128 : k * 128 + 128] = v[4 * k : 4 * k + 4]
-
-    last[1].wait_recv()
-    for cp in copies.values():
-        cp.wait_send()
-    for cp in blocks + [swap] + gates + parts + firsts + rest + last + zed:
-        cp.wait_send()
-
-    @pl.when(mine == 0)
-    def _():
-        for cp in first:
-            cp.wait_send()
-
-    @pl.when(c == 1)
-    def _():
-        to_far.wait_send()
-
-    @pl.when((1 - c) * me.e == 1)
-    def _():
-        half_far.wait_send()
-
-    @pl.when(takes_half == 1)
-    def _():
-        half_twin.wait_send()
-
-    @pl.when(swaps == 1)
-    def _():
-        to_near.wait_send()
+            gate[4 * i : 4 * i + 4, k * 128 : k * 128 + 128] = v[4 * k : 4 * k + 4]
+    cp = pltpu.make_async_copy(gate, o_gate, sem.at[7])
+    cp.start()
+    sent.append(cp)
+    for cp in sent:
+        cp.wait()
 
 
 def on_device(acts, out_grad, saved_proj, weight, shift_scale, gate, image_of):
@@ -634,16 +677,15 @@
     hbm = pl.BlockSpec(memory_space=pl.ANY)
     local = pl.BlockSpec(memory_space=pltpu.VMEM)
     vmem = pltpu.VMEM
-    o_acts, o_w, o_mod, o_gate = pl.pallas_call(
+    mid_acts, mid_w, mid_rec = pl.pallas_call(
         block_kernel,
         out_shape=(
             jax.ShapeDtypeStruct((128, 4096), BF16),
             jax.ShapeDtypeStruct((16, 16, 2048), BF16),
-            jax.ShapeDtypeStruct((64, 2, 4096), F32),
-            jax.ShapeDtypeStruct((64, 2048), F32),
+            jax.ShapeDtypeStruct((16, 20, 16, 128), BF16),
         ),
         in_specs=[pl.BlockSpec(memory_space=pltpu.HBM)] * 6 + [local],
-        out_specs=(local, hbm, local, local),
+        out_specs=(hbm, hbm, hbm),
         scratch_shapes=[
             vmem((128, 4096), BF16), vmem((128, 2048), BF16), vmem((128, 2048), BF16),
             vmem((64, 2048), F32), vmem((64, 2, 4096), F32), vmem((64, 2, 256), F32),
@@ -652,18 +694,19 @@
             vmem((64, 2048), BF16), vmem((16, 64, 128), BF16), vmem((8, 64, 128), BF16),
             vmem((8, 64, 128), BF16), vmem((8, 64, 128), BF16), vmem((256, 2048), BF16),
             vmem((256, 2048), BF16), vmem((16, 128, 256), F32), vmem((16, 128, 256), F32),
-            vmem((16, 128, 256), BF16), vmem((16, 16, 1024), BF16), vmem((16, 16, 1024), BF16),
-            vmem((16, 2, 16, 128), BF16), vmem((16, 2, 16, 1024), BF16),
-            vmem((16, 2, 16, 1024), BF16), vmem((16, 2, 16, 128), BF16),
+            vmem((16, 128, 256), BF16), vmem((16, 16, SPLIT), BF16), vmem((16, 16, WIDE[1]), BF16),
+            vmem((16, 2, 16, 128), BF16), vmem((16, 2, 16, SPLIT), BF16),
+            vmem((16, 2, 16, WIDE[1]), BF16), vmem((16, 2, 16, 128), BF16),
             vmem((128, 4096), BF16), vmem((128, 4096), F32), vmem((16, 2048), BF16),
             vmem((2, 16, 128), BF16), vmem((16, 2, 16, 128), BF16),
-            vmem((16, 20, 16, 128), BF16), vmem((128, 4096), BF16), vmem((16, 128, 256), BF16),
-            vmem((2, 16, 1024), F32), vmem((2, 16, 1024), BF16), vmem((2, 16, 1024), BF16),
-            vmem((2, 16, 1024), F32),
+            vmem((20, 16, 128), BF16), vmem((128, 4096), BF16), vmem((128, 4096), BF16),
+            vmem((16, 128, 256), BF16),
+            vmem((2, 16, max(WIDE)), F32), vmem((2, 16, max(WIDE)), BF16),
+            vmem((2, 16, max(WIDE)), BF16), vmem((2, 16, max(WIDE)), F32),
             dma((n, 3)), dma((n, 3)), dma((n,)), dma((n,)),
             dma((16,)), dma((16,)), dma((16,)), dma((16,)), dma((8,)), dma((8,)),
             dma((4,)), dma((3,)), dma((16,)), dma((16,)), dma((2, 8)), dma((2, 16)),
-            dma((16,)), dma((16,)), dma((15,)), dma((15,)), dma((7,)), dma((7,)), dma((7,)), dma((7,)),
+            dma((16,)), dma((16,)), dma((15,)), dma((15,)), dma((2, 7)), dma((2, 7)), dma((7,)), dma((7,)),
             dma((2,)), dma((2,)), dma((2,)), dma((2,)), dma((7,)),
         ],
         compiler_params=pltpu.CompilerParams(
@@ -671,6 +714,23 @@
         ),
         name="adaln_backward",
     )(acts, out_grad, saved_proj, weight, shift_scale, gate, image_of.reshape(1, 128))
+    o_acts, o_w, o_mod, o_gate = pl.pallas_call(
+        lay_out_kernel,
+        out_shape=(
+            jax.ShapeDtypeStruct((128, 4096), BF16),
+            jax.ShapeDtypeStruct((16, 16, 2048), BF16),
+            jax.ShapeDtypeStruct((64, 2, 4096), F32),
+            jax.ShapeDtypeStruct((64, 2048), F32),
+        ),
+        in_specs=[hbm, hbm, hbm],
+        out_specs=(hbm, hbm, hbm, hbm),
+        scratch_shapes=[
+            vmem((16, 20, 16, 128), BF16), vmem((64, 2, 4096), F32), vmem((64, 2048), F32),
+            vmem((128, 4096), BF16), vmem((16, 16, 2048), BF16), dma((10,)),
+        ],
+        compiler_params=pltpu.CompilerParams(vmem_limit_bytes=60 * 2**20),
+        name="lay_out",
+    )(mid_acts, mid_w, mid_rec)
     return o_acts, o_w.reshape(256, 2048), o_mod, o_gate
 
 

time: 133 us -> 124 us (0.932)
  local copies, waits for them, and re-layouts: 5.61 us -> 0 us
  Pallas kernels: 127 us -> 123 us
    pallas_call x1, Pallas kernels: 127 us -> 119 us  [on_device(): pl.pallas_call(block_kernel, out_shape=(jax.ShapeDtypeStruct((128, 4096),...]
    unnamed x10 -> x0, local copies, waits for them, and re-layouts: 5.61 us -> none
    pallas_call x0 -> x1, Pallas kernels: none -> 3.91 us  [on_device(): pl.pallas_call(lay_out_kernel, out_shape=(jax.ShapeDtypeStruct((128, 4096...]
where the time goes in v4:
time: 124 us
  Pallas kernels  123 us (99%)
    pallas_call x1, Pallas kernels, on_device(): pl.pallas_call(block_kernel, out_shape=(jax.ShapeDtypeStruct((128, 4096),...  119 us
    pallas_call x1, Pallas kernels, on_device(): pl.pallas_call(lay_out_kernel, out_shape=(jax.ShapeDtypeStruct((128, 4096...  3.91 us

profile of v4, /device:TPU:1, one launch (start us, length us, event | category | flops | bytes accessed | tf_op | source)
XLA Modules:
  0.0 123.8 jit_solution(13994605312382456200)
XLA Ops:
  0.6 119.3 %adaln_backward.1 = (bf16[128,4096]{1,0:T(8,128)(2,1)}, bf16[16,16,2048]{2,1,0:T(8,128)(2,1)}, bf16[16,20,16,128]{3,2,1,0:T(8,128)(2,1)}) custom-call(bf16[128,4096]{1,0:T(8,128)(2,1)} %acts.1, bf16[128,2048]{1,0:T(8,128)(2,1)} %og.1, bf16[128,2048]{1,0:T(8,128)(2,1)} %sp.1, bf16[256,2048]{1,0:T(8,128)(2,1)} %w.1, f32[64,2,4096]{2,1,0:T(2,128)} %ss.1, ...), custom_call_target="tpu_custom_call" | custom-call | tf_op jit(solution)/shard_map/adaln_backward/pallas_call | solution.py:680
  119.9 3.9 %lay_out.1 = (bf16[128,4096]{1,0:T(8,128)(2,1)}, bf16[16,16,2048]{2,1,0:T(8,128)(2,1)}, f32[64,2,4096]{2,1,0:T(2,128)}, f32[64,2048]{1,0:T(8,128)}) custom-call(bf16[128,4096]{1,0:T(8,128)(2,1)} %get-tuple-element.11.acts, bf16[16,16,2048]{2,1,0:T(8,128)(2,1)} %get-tuple-element.12.w, bf16[16,20,16,128]{3,2,1,0:T(8,128)(2,1)} %get-tuple-element.13.rec_in), custom_call_target="tpu_custom_call" | custom-call | tf_op jit(solution)/shard_map/lay_out/pallas_call | solution.py:717

commit v5 on v4

--- a/solution.py
+++ b/solution.py
@@ -13,9 +13,9 @@
     (0, 128, (0, 1, 2)),
     (128, 256, (1, 2, 0)),
     (384, 384, (2, 0, 1)),
-    (768, 256, (0, 1, 2)),
-    (1024, 512, (1, 2, 0)),
-    (1536, 512, (2, 0, 1)),
+    (768, 384, (0, 1, 2)),
+    (1152, 512, (1, 2, 0)),
+    (1664, 384, (2, 0, 1)),
 )
 SPLIT = 768
 WIDE = (768, 1280)
@@ -319,13 +319,12 @@
 
     stage(2, 0)
     stage(1, 1)
+    stage(2, 1)
 
     @pl.when(takes_half == 1)
     def _():
         half_far.wait_recv()
         half_twin.start()
-
-    stage(2, 1)
 
     loads[5].wait()
 

time: 124 us -> 123 us (level)
  no operation moved by 1% of the time
where the time goes in v5:
time: 123 us
  Pallas kernels  122 us (99%)
    pallas_call x1, Pallas kernels, on_device(): pl.pallas_call(block_kernel, out_shape=(jax.ShapeDtypeStruct((128, 4096),...  119 us
    pallas_call x1, Pallas kernels, on_device(): pl.pallas_call(lay_out_kernel, out_shape=(jax.ShapeDtypeStruct((128, 4096...  3.91 us

profile of v5, /device:TPU:1, one launch (start us, length us, event | category | flops | bytes accessed | tf_op | source)
XLA Modules:
  0.0 123.1 jit_solution(1839099621402027334)
XLA Ops:
  0.6 118.5 %adaln_backward.1 = (bf16[128,4096]{1,0:T(8,128)(2,1)}, bf16[16,16,2048]{2,1,0:T(8,128)(2,1)}, bf16[16,20,16,128]{3,2,1,0:T(8,128)(2,1)}) custom-call(bf16[128,4096]{1,0:T(8,128)(2,1)} %acts.1, bf16[128,2048]{1,0:T(8,128)(2,1)} %og.1, bf16[128,2048]{1,0:T(8,128)(2,1)} %sp.1, bf16[256,2048]{1,0:T(8,128)(2,1)} %w.1, f32[64,2,4096]{2,1,0:T(2,128)} %ss.1, ...), custom_call_target="tpu_custom_call" | custom-call | tf_op jit(solution)/shard_map/adaln_backward/pallas_call | solution.py:679
  119.2 3.9 %lay_out.1 = (bf16[128,4096]{1,0:T(8,128)(2,1)}, bf16[16,16,2048]{2,1,0:T(8,128)(2,1)}, f32[64,2,4096]{2,1,0:T(2,128)}, f32[64,2048]{1,0:T(8,128)}) custom-call(bf16[128,4096]{1,0:T(8,128)(2,1)} %get-tuple-element.11.acts, bf16[16,16,2048]{2,1,0:T(8,128)(2,1)} %get-tuple-element.12.w, bf16[16,20,16,128]{3,2,1,0:T(8,128)(2,1)} %get-tuple-element.13.rec_in), custom_call_target="tpu_custom_call" | custom-call | tf_op jit(solution)/shard_map/lay_out/pallas_call | solution.py:716
